TPU v7x, 32 devices: a whole 2x2x4 slice. The times are simulated.
32 devices in a mesh: narrow: 4 (over y, x), wide: 8 (over z, core).
Axes of the slice: x: 2, y: 2, z: 4, core: 2. Of those that a mesh axis runs over, the one named last changes fastest.
Arguments:
- tokens: bfloat16 [32768, 1024], P(('narrow', 'wide')), may hold values from -6 to 6
- norm_gains: float32 [2, 1024], replicated, may hold values from 0.25 to 1.75
- norm_biases: float32 [2, 1024], replicated, may hold values from -2 to 2
- w_qkv: bfloat16 [1024, 3072], replicated, may hold values from -0.25 to 0.25
- w_attn_out: bfloat16 [1024, 1024], replicated, may hold values from -0.75 to 0.75
- w_in: bfloat16 [8, 1024, 4096], P('wide'), may hold values from -0.1875 to 0.1875
- w_out: bfloat16 [8, 4096, 1024], P('wide'), may hold values from -0.09375 to 0.09375
- segment_ids: int32 [32, 1024], P(('narrow', 'wide')), may hold values from 0 to 3, never falling along the last dimension, each value on 1 to 512 neighbouring positions
- expert_ids: int32 [32768], P(('narrow', 'wide')), may hold values from 0 to 7, as said below
- slots: int32 [32768], P(('narrow', 'wide')), may hold values from 0 to 144, as said below
- cotangent: bfloat16 [32768, 1024], P(('narrow', 'wide')), may hold values from -6 to 6
Outputs:
- mixed: bfloat16 [32768, 1024], P(('narrow', 'wide'))
- d_tokens: float32 [32768, 1024], P(('narrow', 'wide'))
- d_norm_gains: float32 [2, 1024], P(None, ('narrow', 'wide'))
- d_norm_biases: float32 [2, 1024], P(None, ('narrow', 'wide'))
- d_w_qkv: float32 [1024, 3072], P(None, ('narrow', 'wide'))
- d_w_attn_out: float32 [1024, 1024], P(None, ('narrow', 'wide'))
- d_w_in: float32 [8, 1024, 4096], P('wide', None, 'narrow')
- d_w_out: float32 [8, 4096, 1024], P('wide', 'narrow')
Inputs may be any that keep to these rules, and one draw needn't show every extreme that they name: `expert_ids`: each token's expert, from a hash of the token. The number of earlier tokens of the same device that have the same expert, or 144 where that number is 144 or more (the token is dropped); so the retained tokens of one device and expert hold slots 0, 1, 2, ... without gaps, and on every device some expert fills all 144 slots.
All inputs are finite; a program needn't handle non-finite values.
Results may differ from a plain program's by a relative error of at most 0.012.
The roundings to bfloat16 on the way count: a program that leaves them out, or rounds other values in their place, can miss the bound.
Values may be sent and summed in bfloat16 or wider, within the bound.
No kernel may reach another device: no remote copies, remote signals or barrier semaphores. Data moves between devices by JAX's collectives and lax.ppermute only.
A program may use at most 320 MiB of HBM per device.

v0:
```python
import functools
import itertools

import jax
import jax.numpy as jnp
from jax import lax
from jax.experimental import pallas as pl
from jax.experimental.pallas import tpu as pltpu
from jax.sharding import PartitionSpec as P

HEADS = 16
EPSILON = 1e-05
NEGATIVE = -1e30
BAND = 512
BLOCK = 256
SUB = 512
TILE = 256
SPARE = 16
PARTS = 3
F32 = jnp.float32
BF = jnp.bfloat16
LAST_ROWS = 128
COST_GATE = 6
COST_MIDDLE = 25
PAIRS_FIRST = 5
VMEM_BYTES = 48 * 1024 * 1024


def mm(a, b):
    return lax.dot_general(a, b, (((1,), (0,)), ((), ())), preferred_element_type=F32)


def mm_nt(a, b):
    return lax.dot_general(a, b, (((1,), (1,)), ((), ())), preferred_element_type=F32)


def mm_tn(a, b):
    return lax.dot_general(a, b, (((0,), (0,)), ((), ())), preferred_element_type=F32)


ORDER = []


def call(kernel, grid, in_specs, out_specs, out_shape, scratch=(), prefetch=0, aliases=None, after=(), cost=0):
    count = prefetch + len(in_specs)
    extra = len(after) + len(ORDER)
    order = list(ORDER)
    several = isinstance(out_specs, list)
    outs = len(out_specs) if several else 1

    def body(*refs):
        rest = refs[count + extra :]
        kernel(*refs[:count], *rest[:outs], *rest[outs + 1 :])
        rest[outs][...] = jnp.zeros_like(rest[outs])

    run = pl.pallas_call(
        body,
        grid_spec=pltpu.PrefetchScalarGridSpec(
            num_scalar_prefetch=prefetch,
            grid=grid,
            in_specs=list(in_specs)
            + [pl.BlockSpec(memory_space=pltpu.HBM)] * len(after)
            + [pl.BlockSpec(memory_space=pl.ANY)] * len(ORDER),
            out_specs=[*(out_specs if several else [out_specs]), whole((8, 128))],
            scratch_shapes=list(scratch),
        ),
        out_shape=[*(out_shape if several else [out_shape]), jax.ShapeDtypeStruct((8, 128), F32)],
        input_output_aliases=aliases or {},
        compiler_params=pltpu.CompilerParams(vmem_limit_bytes=VMEM_BYTES),
        cost_estimate=pl.CostEstimate(flops=1 + int(cost * 1.15e9), bytes_accessed=0, transcendentals=0),
    )

    def apply(*args):
        *results, token = run(*args, *[far(a) for a in after], *order)
        ORDER[:] = [token]
        return results if several else results[0]

    return apply


def far(value):
    return pltpu.with_memory_space_constraint(value, pltpu.HBM)


def whole(shape):
    return pl.BlockSpec(shape, lambda *_: (0,) * len(shape))


def normalize(stream):
    average = jnp.mean(stream, axis=-1, keepdims=True)
    centered = stream - average
    inverse = lax.rsqrt(jnp.mean(centered * centered, axis=-1, keepdims=True) + EPSILON)
    return centered * inverse, inverse


def norm_back(unit, inverse, gain, grad):
    scaled = grad * gain
    first = jnp.mean(scaled, axis=-1, keepdims=True)
    second = jnp.mean(scaled * unit, axis=-1, keepdims=True)
    return inverse * (scaled - first - unit * second)


def first_norm_kernel(x_ref, g_ref, b_ref, n_ref):
    unit, _inverse = normalize(x_ref[...].astype(F32))
    n_ref[...] = (unit * g_ref[0:1, :] + b_ref[0:1, :]).astype(BF)


def first_norm(tokens, gains, biases, after=(), cost=0):
    rows, dim = tokens.shape
    block = pl.BlockSpec((256, dim), lambda i: (i, 0))
    return call(
        first_norm_kernel,
        (rows // 256,),
        [block, whole(gains.shape), whole(biases.shape)],
        block,
        pltpu.HBM((rows, dim), BF),
        after=after,
        cost=cost,
    )(far(tokens), far(gains), far(biases))


def project_kernel(n_ref, w_ref, p_ref):
    p_ref[...] = mm(n_ref[...], w_ref[...]).astype(BF)


def project(normed, w_qkv, after=(), cost=0):
    rows, dim = normed.shape
    cols = w_qkv.shape[1]
    tile = 768
    return call(
        project_kernel,
        (cols // tile,),
        [whole((rows, dim)), pl.BlockSpec((dim, tile), lambda j: (0, j))],
        pl.BlockSpec((rows, tile), lambda j: (0, j)),
        jax.ShapeDtypeStruct((rows, cols), BF),
        after=after,
        cost=cost,
    )(far(normed), far(w_qkv))


def fill_masks(col_ref, fq_ref, fk_ref, tri_ref, head_dim):
    length = col_ref.shape[0]
    doc = lax.broadcasted_iota(jnp.int32, fq_ref.shape, 1) % head_dim
    same = doc == col_ref[...]
    fq_ref[...] = jnp.where(same, 1.0, 0.0).astype(BF)
    fk_ref[...] = jnp.where(same, 0.0, NEGATIVE).astype(BF)
    key_pos = lax.broadcasted_iota(jnp.int32, tri_ref.shape, 0)
    query_pos = lax.broadcasted_iota(jnp.int32, tri_ref.shape, 1)
    tri_ref[...] = jnp.where(key_pos <= query_pos, 0.0, NEGATIVE).astype(F32)


def lanes_of(shape, head, head_dim):
    lane = lax.broadcasted_iota(jnp.int32, shape, 1)
    return (lane >= head * head_dim) & (lane < (head + 1) * head_dim)


def attn_fwd_kernel(head_dim, col_ref, q_ref, k_ref, v_ref, o_ref, ol_ref, lse_ref, fq_ref, fk_ref, tri_ref, vt_ref, qh_ref, kh_ref):
    length, pair = q_ref.shape
    scale = head_dim**-0.5
    per = pair // head_dim

    @pl.when(pl.program_id(0) == 0)
    def _():
        fill_masks(col_ref, fq_ref, fk_ref, tri_ref, head_dim)
        vt_ref[...] = jnp.ones_like(vt_ref)

    value_t = v_ref[...].T
    query = q_ref[...] * BF(scale)
    for head in range(per):
        inside = lanes_of(query.shape, head, head_dim)
        vt_ref[head, :head_dim, :] = value_t[head * head_dim : (head + 1) * head_dim, :]
        qh_ref[head] = jnp.where(inside, query, fq_ref[...])
        kh_ref[head] = jnp.where(inside, k_ref[...], fk_ref[...])
    def first_stage(q_first):
        k_first = max(0, q_first - BAND)
        allparts = [[] for _ in range(per)]
        for k_at in range(k_first, q_first + BLOCK, BLOCK):
            for head in range(per):
                scores = mm_nt(kh_ref[head, k_at : k_at + BLOCK, :], qh_ref[head, q_first : q_first + BLOCK, :])
                if k_at == q_first:
                    scores = scores + tri_ref[...]
                allparts[head].append(scores)
        tops = [functools.reduce(jnp.maximum, [jnp.max(p, axis=0, keepdims=True) for p in parts]) for parts in allparts]
        return allparts, tops

    def second_stage(q_first, allparts, tops):
        k_first = max(0, q_first - BAND)
        q_at = slice(q_first, q_first + BLOCK)
        totals = [None] * per
        for i in range(len(allparts[0])):
            k_at = k_first + i * BLOCK
            for head in range(per):
                prob = jnp.exp(allparts[head][i] - tops[head]).astype(BF)
                part = mm(vt_ref[head, :, k_at : k_at + BLOCK], prob)
                totals[head] = part if totals[head] is None else totals[head] + part
        outs = []
        for head in range(per):
            total = totals[head]
            sums = total[head_dim : head_dim + 1, :]
            outs.append(total[:head_dim, :] / sums)
            lse_ref[0, head : head + 1, q_at] = tops[head] + jnp.log(sums)
        o_ref[q_at, :], ol_ref[q_at, :] = in_parts(jnp.concatenate(outs, axis=0).T, 2)

    firsts = list(range(0, length, BLOCK))
    ahead = first_stage(firsts[0])
    for i, q_first in enumerate(firsts):
        now = ahead
        if i + 1 < len(firsts):
            ahead = first_stage(firsts[i + 1])
        second_stage(q_first, *now)


def attn_fwd(projected, doc_col, head_dim, cost=0):
    length = projected.shape[0]
    width = projected.shape[1] // 3
    pair = 128
    pairs = width // pair
    per = pair // head_dim
    specs = [pl.BlockSpec((length, pair), functools.partial(lambda s, j: (0, s * pairs + j), s)) for s in range(3)]
    return call(
        functools.partial(attn_fwd_kernel, head_dim),
        (pairs,),
        [whole(doc_col.shape)] + specs,
        [pl.BlockSpec((length, pair), lambda j: (0, j))] * 2 + [pl.BlockSpec((1, per, length), lambda j: (j, 0, 0))],
        [
            jax.ShapeDtypeStruct((length, width), BF),
            pltpu.HBM((length, width), BF),
            pltpu.HBM((pairs, per, length), F32),
        ],
        scratch=[
            pltpu.VMEM((length, pair), BF),
            pltpu.VMEM((length, pair), BF),
            pltpu.VMEM((BLOCK, BLOCK), F32),
            pltpu.VMEM((per, head_dim + 16, length), BF),
            pltpu.VMEM((per, length, pair), BF),
            pltpu.VMEM((per, length, pair), BF),
        ],
        cost=cost,
    )(doc_col, projected, projected, projected)


def in_parts(x, count):
    parts = []
    for _ in range(count):
        parts.append(x.astype(BF))
        x = x - parts[-1].astype(F32)
    return parts


def attn_bwd_kernel(head_dim, col_ref, q_ref, k_ref, v_ref, o_ref, ol_ref, do_ref, lse_ref, g_ref, gt_ref,
                    fq_ref, fk_ref, tri_ref, qx, kx, vx, dox, qm, dom, dk_sum, dv_sum):
    length, pair = q_ref.shape
    scale = head_dim**-0.5
    per = pair // head_dim

    @pl.when(pl.program_id(0) == 0)
    def _():
        fill_masks(col_ref, fq_ref, fk_ref, tri_ref, head_dim)

    key_t = (k_ref[...] * BF(scale)).T
    query = q_ref[...] * BF(scale)
    grad = do_ref[...]
    lane = lax.broadcasted_iota(jnp.int32, (length, pair), 1)
    zero = jnp.zeros_like(query)
    one = jnp.ones_like(query)
    lse_rows = jnp.concatenate([lse_ref[0], jnp.zeros((8 - per, length), F32)], axis=0)
    lse_cols = lse_rows.T
    product = grad.astype(F32) * (o_ref[...].astype(F32) + ol_ref[...].astype(F32))
    for head in range(per):
        inside = lanes_of(query.shape, head, head_dim)
        slots = [lane == (1 - head) * head_dim + head_dim // 2 + i for i in range(PARTS)]
        some = functools.reduce(jnp.logical_or, slots)
        delta = jnp.sum(jnp.where(inside, product, 0.0), axis=1, keepdims=True)

        def spread(column, rest):
            for slot, part in zip(slots, in_parts(-column, PARTS)):
                rest = jnp.where(slot, part, rest)
            return rest

        qm[head] = jnp.where(inside, query, zero)
        dom[head] = jnp.where(inside, grad, zero)
        qx[head] = jnp.where(inside, query, spread(lse_cols[:, head : head + 1], fq_ref[...]))
        kx[head] = jnp.where(inside, k_ref[...], jnp.where(some, one, fk_ref[...]))
        vx[head] = jnp.where(inside, v_ref[...], jnp.where(some, one, zero))
        dox[head] = jnp.where(inside, grad, spread(delta, zero))
    dk_sum[...] = jnp.zeros_like(dk_sum)
    dv_sum[...] = jnp.zeros_like(dv_sum)
    for q_first in range(0, length, BLOCK):
        q_at = slice(q_first, q_first + BLOCK)
        dq_parts = [None] * per
        for k_first in range(max(0, q_first - BAND), q_first + BLOCK, BLOCK):
            k_at = slice(k_first, k_first + BLOCK)
            scores = [mm_nt(kx[h, k_at, :], qx[h, q_at, :]) for h in range(per)]
            prob_grads = [mm_nt(vx[h, k_at, :], dox[h, q_at, :]) for h in range(per)]
            if k_first == q_first:
                scores = [s + tri_ref[...] for s in scores]
            probs = [jnp.exp(s) for s in scores]
            score_grads = [(p * d).astype(BF) for p, d in zip(probs, prob_grads)]
            probs = [p.astype(BF) for p in probs]
            dv_sum[k_at, :] += mm(
                jnp.concatenate(probs, axis=1), jnp.concatenate([dom[h, q_at, :] for h in range(per)], axis=0)
            )
            dk_sum[k_at, :] += mm(
                jnp.concatenate(score_grads, axis=1), jnp.concatenate([qm[h, q_at, :] for h in range(per)], axis=0)
            )
            for h in range(per):
                one = mm(key_t[h * head_dim : (h + 1) * head_dim, k_at], score_grads[h])
                dq_parts[h] = one if dq_parts[h] is None else dq_parts[h] + one
        dq_t = jnp.concatenate(dq_parts, axis=0)
        gt_ref[0, :, q_at] = dq_t.astype(BF)
        g_ref[0, q_at, :] = dq_t.T.astype(BF)
    for i, ref in ((1, dk_sum), (2, dv_sum)):
        low = ref[...].astype(BF)
        g_ref[i] = low
        gt_ref[i] = low.T


def attn_bwd(projected, mixed_heads, mixed_low, grad_heads, log_total, doc_col, head_dim, first, steps, held=(), after=(), cost=0):
    length = projected.shape[0]
    width = projected.shape[1] // 3
    pair = 128
    pairs = width // pair
    per = pair // head_dim
    specs = [
        pl.BlockSpec((length, pair), functools.partial(lambda s, j: (0, s * pairs + first + j), s)) for s in range(3)
    ]
    held = list(held)
    count = len(held)
    kernel = functools.partial(attn_bwd_kernel, head_dim)
    one = pl.BlockSpec((length, pair), lambda j: (0, first + j))
    return call(
        lambda *refs: kernel(*refs[:8], *refs[8 + count :]),
        (steps,),
        [whole(doc_col.shape)] + specs + [one, one, one, pl.BlockSpec((1, per, length), lambda j: (first + j, 0, 0))]
        + [pl.BlockSpec(memory_space=pltpu.HBM)] * count,
        [
            pl.BlockSpec((3, length, pair), lambda j: (0, 0, first + j)),
            pl.BlockSpec((3, pair, length), lambda j: (0, first + j, 0)),
        ],
        [pltpu.HBM((3, length, width), BF), pltpu.HBM((3, width, length), BF)],
        scratch=[
            pltpu.VMEM((length, pair), BF),
            pltpu.VMEM((length, pair), BF),
            pltpu.VMEM((BLOCK, BLOCK), F32),
        ]
        + [pltpu.VMEM((per, length, pair), BF)] * 6
        + [pltpu.VMEM((length, pair), F32)] * 2,
        aliases={8 + i: i for i in range(count)},
        after=after,
        cost=cost,
    )(doc_col, *[far(a) for a in (projected, projected, projected, mixed_heads, mixed_low, grad_heads, log_total)], *held)


def middle_kernel(x_ref, h_ref, w_ref, g_ref, b_ref, *refs):
    m_ref, s_ref = refs[-2:]
    middle = x_ref[...].astype(F32) + mm(h_ref[...], w_ref[...])
    m_ref[...] = middle
    unit, _inverse = normalize(middle)
    s_ref[...] = (unit * g_ref[1:2, :] + b_ref[1:2, :]).astype(BF)


def make_middle(tokens, mixed_heads, w_attn_out, gains, biases, first, count, held=(), after=(), cost=0):
    rows, dim = tokens.shape
    tile = min(count, 448)
    at = first // tile
    block = pl.BlockSpec((tile, dim), lambda i: (at + i, 0))
    held = list(held)
    return call(
        middle_kernel,
        (count // tile,),
        [block, block, whole(w_attn_out.shape), whole(gains.shape), whole(biases.shape)]
        + [pl.BlockSpec(memory_space=pltpu.HBM)] * len(held),
        [block, pl.BlockSpec((tile, dim), lambda i: (i, 0))],
        [pltpu.HBM((rows, dim), F32), jax.ShapeDtypeStruct((count, dim), BF)],
        aliases={5: 0} if held else None,
        after=after,
        cost=cost,
    )(far(tokens), mixed_heads, far(w_attn_out), far(gains), far(biases), *held)


def dispatch_kernel(slots, added, *refs):
    o_refs = refs[4 + added :]
    count = slots * (o_refs[0].shape[0] // (2 * slots)) * len(o_refs)
    for side in range(2):
        place, rows = refs[side], refs[2 + side]
        slot = lax.broadcasted_iota(jnp.int32, (count, rows.shape[0]), 0)
        low = mm(jnp.where(slot == place[...], 1.0, 0.0).astype(BF), rows[...]).astype(BF)
        for i, ref in enumerate(o_refs):
            each = count // len(o_refs)
            at = slice(side * each, (side + 1) * each)
            part = low[i * each : (i + 1) * each]
            ref[at, :] = part + refs[4 + i][at, :] if added else part


def dispatch_rows(places, rows, positions, slots, added=(), after=(), cost=0):
    dim = rows[0].shape[1]
    count = positions if slots % 16 == 0 else 1
    shape = (2 * slots * (positions // count), dim)
    return call(
        functools.partial(dispatch_kernel, slots, len(added)),
        (1,),
        [whole(a.shape) for a in [*places, *rows]] + [whole(shape)] * len(added),
        [whole(shape)] * count,
        [jax.ShapeDtypeStruct(shape, BF)] * count,
        after=after,
        cost=cost,
    )(*places, *rows, *added)


def dispatch_side_kernel(positions, place_ref, x_ref, *refs):
    o_refs = refs[-positions:]
    slots = o_refs[0].shape[0]
    slot = lax.broadcasted_iota(jnp.int32, (positions * slots, x_ref.shape[0]), 0)
    low = mm(jnp.where(slot == place_ref[...], 1.0, 0.0).astype(BF), x_ref[...]).astype(BF)
    for i, ref in enumerate(o_refs):
        ref[...] = low[i * slots : (i + 1) * slots]


def dispatch_side(place, rows, positions, slots, side, held=(), after=(), cost=0):
    dim = rows.shape[1]
    held = list(held)
    return call(
        functools.partial(dispatch_side_kernel, positions),
        (1,),
        [whole(place.shape), whole(rows.shape)] + [pl.BlockSpec(memory_space=pltpu.HBM)] * len(held),
        [pl.BlockSpec((slots, dim), lambda i: (side, 0))] * positions,
        [pltpu.HBM((2 * slots, dim), BF)] * positions,
        aliases={2 + i: i for i in range(len(held))},
        after=after,
        cost=cost,
    )(place, rows, *held)


def separate(out, positions, slots):
    if len(out) > 1:
        return out
    sides = out[0].reshape(2, positions, slots, out[0].shape[1])
    return [sides[:, p].reshape(2 * slots, out[0].shape[1]) for p in range(positions)]


def fill(joined_ref, block_refs):
    at = 0
    for ref in block_refs:
        joined_ref[at : at + ref.shape[0], :] = ref[...]
        at += ref.shape[0]


def pick_rows(place, back):
    slot = lax.broadcasted_iota(jnp.int32, (place.shape[0], back.shape[0]), 1)
    return mm(jnp.where(slot == place, 1.0, 0.0).astype(BF), back)


def mixed_kernel(count, place_ref, m_ref, *refs):
    o_ref, joined_ref = refs[count:]

    @pl.when(pl.program_id(0) == 0)
    def _():
        fill(joined_ref, refs[:count])

    o_ref[...] = (m_ref[...] + pick_rows(place_ref[...], joined_ref[...])).astype(BF)


def make_mixed(place_col, middle, back, after=(), cost=0):
    rows, dim = middle.shape
    tile = 256
    total = sum(n for _, n in back)
    block = pl.BlockSpec((tile, dim), lambda i: (i, 0))
    return call(
        functools.partial(mixed_kernel, len(back)),
        (rows // tile,),
        [pl.BlockSpec((tile, 1), lambda i: (i, 0)), block] + [whole((n, dim)) for _, n in back],
        block,
        jax.ShapeDtypeStruct((rows, dim), BF),
        scratch=[pltpu.VMEM((total, dim), BF)],
        after=after,
        cost=cost,
    )(place_col, far(middle), *[far(b) for b, _ in back])


def second_back_kernel(count, place_ref, m_ref, c_ref, w_ref, g_ref, *refs):
    gm_ref, gat_ref, gh_ref, sums_ref, joined_ref = refs[count:]

    @pl.when(pl.program_id(0) == 0)
    def _():
        fill(joined_ref, refs[:count])

    grad_sent = pick_rows(place_ref[...], joined_ref[...])
    unit, inverse = normalize(m_ref[...])
    grad_middle = c_ref[...].astype(F32) + norm_back(unit, inverse, g_ref[1:2, :], grad_sent)
    gm_ref[...] = grad_middle
    grad_attn = grad_middle.astype(BF)
    gat_ref[...] = grad_attn.T
    gh_ref[...] = mm_nt(grad_attn, w_ref[...]).astype(BF)
    sums = jnp.concatenate(
        [jnp.sum(grad_sent * unit, axis=0, keepdims=True), jnp.sum(grad_sent, axis=0, keepdims=True)], axis=0
    )

    @pl.when(pl.program_id(0) == 0)
    def _():
        sums_ref[...] = sums

    @pl.when(pl.program_id(0) > 0)
    def _():
        sums_ref[...] += sums


def second_back(place_col, middle, cotangent, back, w_attn_out, gains, after=(), cost=0):
    rows, dim = middle.shape
    tile = 256
    total = sum(n for _, n in back)
    block = pl.BlockSpec((tile, dim), lambda i: (i, 0))
    return call(
        functools.partial(second_back_kernel, len(back)),
        (rows // tile,),
        [pl.BlockSpec((tile, 1), lambda i: (i, 0)), block, block, whole(w_attn_out.shape), whole(gains.shape)]
        + [whole((n, dim)) for _, n in back],
        [block, pl.BlockSpec((dim, tile), lambda i: (0, i)), block, whole((2, dim))],
        [
            pltpu.HBM((rows, dim), F32),
            pltpu.HBM((dim, rows), BF),
            pltpu.HBM((rows, dim), BF),
            jax.ShapeDtypeStruct((2, dim), F32),
        ],
        scratch=[pltpu.VMEM((total, dim), BF)],
        after=after,
        cost=cost,
    )(place_col, far(middle), far(cotangent), far(w_attn_out), far(gains), *[far(b) for b, _ in back])


def first_back_kernel(x_ref, gm_ref, d_ref, w_ref, g_ref, dx_ref, sums_ref):
    dim = x_ref.shape[1]
    grad_normed = mm_nt(d_ref[0], w_ref[:, :dim])
    grad_normed += mm_nt(d_ref[1], w_ref[:, dim : 2 * dim])
    grad_normed += mm_nt(d_ref[2], w_ref[:, 2 * dim :])
    unit, inverse = normalize(x_ref[...].astype(F32))
    dx_ref[...] = gm_ref[...] + norm_back(unit, inverse, g_ref[0:1, :], grad_normed)
    sums = jnp.concatenate(
        [jnp.sum(grad_normed * unit, axis=0, keepdims=True), jnp.sum(grad_normed, axis=0, keepdims=True)], axis=0
    )

    @pl.when(pl.program_id(0) == 0)
    def _():
        sums_ref[...] = sums

    @pl.when(pl.program_id(0) > 0)
    def _():
        sums_ref[...] += sums


def first_back(tokens, grad_middle, grads, w_qkv, gains, after=(), cost=0):
    rows, dim = tokens.shape
    tile = 256
    block = pl.BlockSpec((tile, dim), lambda i: (i, 0))
    return call(
        first_back_kernel,
        (rows // tile,),
        [
            block,
            block,
            pl.BlockSpec((3, tile, dim), lambda i: (0, i, 0)),
            whole(w_qkv.shape),
            whole(gains.shape),
        ],
        [block, whole((2, dim))],
        [jax.ShapeDtypeStruct((rows, dim), F32), jax.ShapeDtypeStruct((2, dim), F32)],
        after=after,
        cost=cost,
    )(far(tokens), far(grad_middle), far(grads), far(w_qkv), far(gains))


def grad_hidden_kernel(count, wo_ref, *refs):
    gh_ref, joined_ref = refs[-2:]

    @pl.when(pl.program_id(0) == 0)
    def _():
        fill(joined_ref, refs[:count])

    gh_ref[...] = mm_nt(joined_ref[...], wo_ref[...]).astype(BF)


def grad_hidden(grads, w_out, first, total, held=(), after=(), cost=0):
    rows = sum(g.shape[0] for g in grads)
    units, dim = w_out.shape
    tile = 1024
    at = first // rows
    held = list(held)
    return call(
        functools.partial(grad_hidden_kernel, len(grads)),
        (units // tile,),
        [pl.BlockSpec((tile, dim), lambda j: (j, 0))]
        + [whole(g.shape) for g in grads]
        + [pl.BlockSpec(memory_space=pltpu.HBM)] * len(held),
        pl.BlockSpec((rows, tile), lambda j: (at, j)),
        pltpu.HBM((total, units), BF),
        scratch=[pltpu.VMEM((rows, dim), BF)],
        aliases={1 + len(grads) + i: i for i in range(len(held))},
        after=after,
        cost=cost,
    )(far(w_out), *grads, *held)


def expert_kernel(count, aliased, wi_ref, gh_ref, *refs):
    blocks = refs[:count]
    outs = refs[count + aliased :]
    h_ref, gp_ref = outs[:2]
    gr_refs = outs[2:-2]
    joined_ref, gr_sum = outs[-2:]
    step = pl.program_id(0)

    @pl.when(step == 0)
    def _():
        fill(joined_ref, blocks)
        gr_sum[...] = jnp.zeros_like(gr_sum)

    slope = 0.7978845608028654

    def preact_of(first):
        return mm(joined_ref[...], wi_ref[:, first : first + SUB])

    def add_rows_grad(first):
        cols = slice(first, first + SUB)
        gr_sum[...] += mm_nt(gp_ref[:, cols], wi_ref[:, cols])

    firsts = list(range(0, wi_ref.shape[1], SUB))
    ahead = preact_of(firsts[0])
    for i, first in enumerate(firsts):
        preact = ahead
        if i + 1 < len(firsts):
            ahead = preact_of(firsts[i + 1])
        if i > 0:
            add_rows_grad(firsts[i - 1])
        cols = slice(first, first + SUB)
        square = preact * preact
        tanh = jnp.tanh(preact * (slope + (slope * 0.044715) * square))
        half = 0.5 + 0.5 * tanh
        hidden = preact * half
        gate = half + hidden * (1.0 - tanh) * (slope + (3.0 * slope * 0.044715) * square)
        h_ref[:, cols] = hidden.astype(BF)
        gp_ref[:, cols] = (gate * gh_ref[:, cols].astype(F32)).astype(BF)
    add_rows_grad(firsts[-1])

    @pl.when(step == pl.num_programs(0) - 1)
    def _():
        at = 0
        for ref in gr_refs:
            ref[...] = gr_sum[at : at + ref.shape[0], :].astype(BF)
            at += ref.shape[0]


def expert(blocks, gh, w_in, first, held=(), out_rows=None, after=(), cost=0):
    count = sum(b.shape[0] for b in blocks)
    dim, units = w_in.shape
    tile = 2048
    at = first // count
    act = pl.BlockSpec((count, tile), lambda j: (at, j))
    shape = pltpu.HBM(gh.shape, BF)
    held = list(held)
    pieces = out_rows or [b.shape[0] for b in blocks]
    return call(
        functools.partial(expert_kernel, len(blocks), len(held)),
        (units // tile,),
        [pl.BlockSpec((dim, tile), lambda j: (0, j)), act]
        + [whole(b.shape) for b in blocks]
        + [pl.BlockSpec(memory_space=pltpu.HBM)] * len(held),
        [act, act] + [whole((n, dim)) for n in pieces],
        [shape, shape] + [pltpu.HBM((n, dim), BF) for n in pieces],
        scratch=[pltpu.VMEM((count, dim), BF), pltpu.VMEM((count, dim), F32)],
        aliases={2 + len(blocks) + i: i for i in range(len(held))},
        after=after,
        cost=cost,
    )(w_in, gh, *blocks, *held)


def turn_kernel(count, *refs):
    o_ref, joined_ref = refs[count:]
    fill(joined_ref, refs[:count])
    o_ref[...] = joined_ref[...].T


def turned(blocks, after=(), cost=0):
    total = sum(b.shape[0] for b in blocks)
    dim = blocks[0].shape[1]
    return call(
        functools.partial(turn_kernel, len(blocks)),
        (1,),
        [whole(b.shape) for b in blocks],
        whole((dim, total)),
        pltpu.HBM((dim, total), BF),
        scratch=[pltpu.VMEM((total, dim), BF)],
        after=after,
        cost=cost,
    )(*blocks)


def produced_kernel(h_ref, wo_ref, *refs):
    o_refs, total_ref = refs[:-1], refs[-1]
    step = pl.program_id(0)
    part = mm(h_ref[...], wo_ref[...])

    @pl.when(step == 0)
    def _():
        total_ref[...] = part

    @pl.when(step > 0)
    def _():
        total_ref[...] += part

    @pl.when(step == pl.num_programs(0) - 1)
    def _():
        at = 0
        for ref in o_refs:
            ref[...] = total_ref[at : at + ref.shape[0], :].astype(BF)
            at += ref.shape[0]


def make_produced(hidden, w_out, pieces, after=(), cost=0):
    rows, units = hidden.shape
    dim = w_out.shape[1]
    tile = 1024
    return call(
        produced_kernel,
        (units // tile,),
        [pl.BlockSpec((rows, tile), lambda j: (0, j)), pl.BlockSpec((tile, dim), lambda j: (j, 0))],
        [whole((n, dim)) for n in pieces],
        [jax.ShapeDtypeStruct((n, dim), BF) for n in pieces],
        scratch=[pltpu.VMEM((rows, dim), F32)],
        after=after,
        cost=cost,
    )(hidden, w_out)


def halves_kernel(count, slots, *refs):
    o_ref = refs[-1]
    for i in range(count):
        o_ref[i * slots : (i + 1) * slots, :] = refs[i][...]


def second_halves(blocks, slots, after=(), cost=0):
    dim = blocks[0].shape[1]
    count = len(blocks)
    return call(
        functools.partial(halves_kernel, count, slots),
        (1,),
        [pl.BlockSpec((slots, dim), lambda i: (1, 0))] * count,
        whole((count * slots, dim)),
        jax.ShapeDtypeStruct((count * slots, dim), BF),
        after=after,
        cost=cost,
    )(*blocks)


def add_kernel(count, *refs):
    outs = refs[2 * count :]
    rows = refs[0].shape[1]
    for i in range(count):
        o_ref, at = outs[i // 2], i % 2
        o_ref[at, :rows, :] = (refs[2 * i][0].astype(F32) + refs[2 * i + 1][0].astype(F32)).astype(BF)
        o_ref[at, rows:, :] = jnp.zeros((o_ref.shape[1] - rows, o_ref.shape[2]), BF)


def add_second(pairs, after=(), cost=0):
    _, rows, cols = pairs[0][0].shape
    steps = rows // TILE
    each = TILE + SPARE
    count = len(pairs)
    block = pl.BlockSpec((1, TILE, cols), lambda i: (1, i, 0))
    return call(
        functools.partial(add_kernel, count),
        (steps,),
        [block] * (2 * count),
        [pl.BlockSpec((2, each, cols), lambda i: (0, i, 0))] * (count // 2),
        [pltpu.HBM((2, steps * each, cols), BF)] * (count // 2),
        after=after,
        cost=cost,
    )(*[far(a) for pair in pairs for a in pair])


def stack_kernel(a_ref, b_ref, o_ref):
    o_ref[0:1, :] = a_ref[0:1, :]
    o_ref[1:2, :] = b_ref[0:1, :]
    o_ref[2:3, :] = a_ref[1:2, :]
    o_ref[3:4, :] = b_ref[1:2, :]


def stack_sums(first, second, after=(), cost=0):
    _, dim = first.shape
    return call(
        stack_kernel,
        (1,),
        [whole(first.shape), whole(second.shape)],
        whole((4, dim)),
        jax.ShapeDtypeStruct((4, dim), F32),
        after=after,
        cost=cost,
    )(first, second)


def weights_kernel(count, puts, table_ref, l_ref, r_ref, *refs):
    half = l_ref.shape[0] // 2
    outs = refs[count:]

    for step, (first, last) in enumerate(puts):

        @pl.when(pl.program_id(0) == step)
        def _(first=first, last=last):
            outs[first][0] = mm(l_ref[:half, :], r_ref[...]).astype(BF)
            outs[last][0] = mm(l_ref[half:, :], r_ref[...]).astype(BF)


def weight_parts(left, right, table, count=4, held=(), after=(), cost=0):
    dim, depth = left.shape
    quarter = right.shape[1] // 4
    half = pltpu.HBM((2, dim // 2, quarter), BF)
    held = list(held)

    def part(until):
        return pl.BlockSpec((1, dim // 2, quarter), lambda i, t: (jnp.where(i <= until, 1, 0), 0, 0))

    if held:
        puts, specs = [(0, 1)], [part(-1), part(-1)]
    else:
        puts, specs = [(0, 1), (0, 3), (2, 1), (2, 3)][:count], [part(0), part(1), part(2), part(2)]
    steps = len(puts)
    return call(
        functools.partial(weights_kernel, len(held), puts),
        (steps,),
        [whole(left.shape), pl.BlockSpec((depth, quarter), lambda i, t: (0, t[i + (3 if held else 0)]))]
        + [pl.BlockSpec(memory_space=pltpu.HBM)] * len(held),
        specs,
        [half] * len(specs),
        prefetch=1,
        aliases={3 + i: i for i in range(len(held))},
        after=after,
        cost=cost,
    )(table, far(left), right, *held)


def joint_kernel(bit_ref, g_ref, ga_ref, n_ref, h_ref, *out_refs):
    low = bit_ref[0] == 0
    for side in range(2):
        keep_ref, send_ref = out_refs[2 * side : 2 * side + 2]
        own = 2 * keep_ref.shape[0]
        cols = keep_ref.shape[2]
        at = slice(side * cols, (side + 1) * cols)
        qkv_part = mm(g_ref[...], n_ref[:, at]).reshape(own, g_ref.shape[0] // own, cols)
        out_part = mm(ga_ref[...], h_ref[:, at]).reshape(own, ga_ref.shape[0] // own, cols)
        both = jnp.concatenate([qkv_part, out_part], axis=1).astype(BF)
        both = both.reshape(own // 2, 2, *both.shape[1:])
        keep_ref[...] = jnp.where(low, both[:, 0], both[:, 1])
        send_ref[...] = jnp.where(low, both[:, 1], both[:, 0])


def joint(grads_t, grad_attn_t, normed, mixed_heads, bit, owners, after=(), cost=0):
    rows, dim = normed.shape
    steps = 4
    cols = dim // 2
    own = owners // steps
    qkv_rows = grads_t.shape[0] // steps
    out_rows = grad_attn_t.shape[0] // steps
    each = (qkv_rows + out_rows) // own
    block = pl.BlockSpec((own // 2, each, cols), lambda i, _: (i, 0, 0))
    return call(
        joint_kernel,
        (steps,),
        [
            pl.BlockSpec((qkv_rows, rows), lambda i, _: (i, 0)),
            pl.BlockSpec((out_rows, rows), lambda i, _: (i, 0)),
            whole((rows, dim)),
            whole((rows, dim)),
        ],
        [block] * 4,
        [pltpu.HBM((owners // 2, each, cols), BF)] * 4,
        prefetch=1,
        after=after,
        cost=cost,
    )(bit, far(grads_t), far(grad_attn_t), far(normed), far(mixed_heads))


def add_half_kernel(shapes, *refs):
    refs = refs[len(shapes) :]
    outs = refs[2 * sum(shapes) :]
    for parts, o_ref in zip(shapes, outs):
        cols = refs[0].shape[-1]
        for i in range(parts):
            mine, got = refs[:2]
            refs = refs[2:]
            o_ref[..., i * cols : (i + 1) * cols] = (mine[...].astype(F32) + got[...].astype(F32)).astype(BF)


def add_half(sets, flip, far_in=False, far_out=False, after=(), cost=0):
    in_specs, out_specs, out_shape, args, shapes = [], [], [], [], []
    for number, (pairs, bit, inner) in enumerate(sets):
        count, rows, cols = pairs[0][0].shape
        outer = count // (2 * inner)
        inner_each = min(inner, 4)
        outer_each = min(outer, 4 // inner_each)
        inner_steps = inner // inner_each
        steps = outer // outer_each * inner_steps

        def at_bit(i, *b, number=number, inner_steps=inner_steps):
            return (i // inner_steps, b[number][0] ^ flip, i % inner_steps, 0, 0)

        def at(i, *b, inner_steps=inner_steps):
            return (i // inner_steps, i % inner_steps, 0, 0)

        in_specs += [pl.BlockSpec((outer_each, None, inner_each, rows, cols), at_bit)] * (2 * len(pairs))
        out_specs.append(pl.BlockSpec((outer_each, inner_each, rows, len(pairs) * cols), at))
        out_shape.append((pltpu.HBM if far_out else jax.ShapeDtypeStruct)((outer, inner, rows, len(pairs) * cols), BF))
        for mine, got in pairs:
            mine, got = [a.reshape(outer, 2, inner, rows, cols) for a in (mine, got)]
            args += [far(mine) if far_in else mine, got]
        shapes.append(len(pairs))
    results = call(
        functools.partial(add_half_kernel, shapes),
        (steps,),
        in_specs,
        out_specs,
        out_shape,
        prefetch=len(sets),
        after=after,
        cost=cost,
    )(*[bit for _, bit, _ in sets], *args)
    return [r.reshape(-1, *r.shape[2:]) for r in results]


def add_rows_kernel(count, *refs):
    total = refs[0][...]
    for i in range(1, count):
        total += refs[i][...]
    refs[count][...] = total


def add_rows(values, after=(), cost=0):
    shape = values[0].shape
    return call(
        functools.partial(add_rows_kernel, len(values)),
        (1,),
        [whole(shape)] * len(values),
        whole(shape),
        jax.ShapeDtypeStruct(shape, F32),
        after=after,
        cost=cost,
    )(*values)


def finish_kernel(turn, *refs):
    o_ref = refs[-1]
    rows = refs[0].shape[1]
    total = refs[0][0].astype(F32) + refs[1][0].astype(F32) + refs[2][0, :rows].astype(F32)
    o_ref[...] = total.T if turn else total


def finish(keep, got, last, which, turn, side, held=None, after=(), cost=0):
    _, rows, cols = keep.shape
    tile = TILE
    block = pl.BlockSpec((1, tile, cols), lambda i: (0, i, 0))
    steps = rows // tile
    shape = (cols, 2 * rows) if turn else (2 * rows, cols)
    out = (
        pl.BlockSpec((cols, tile), lambda i: (0, side * steps + i))
        if turn
        else pl.BlockSpec((tile, cols), lambda i: (side * steps + i, 0))
    )
    more = [] if held is None else [held]
    count = len(more)

    def body(*refs):
        finish_kernel(turn, *refs[:3], refs[3 + count])

    return call(
        body,
        (steps,),
        [block] * 2
        + [pl.BlockSpec((1, tile + SPARE, cols), lambda i: (which, i, 0))]
        + [pl.BlockSpec(memory_space=pltpu.HBM)] * count,
        out,
        pltpu.HBM(shape, F32),
        aliases={3: 0} if more else None,
        after=after,
        cost=cost,
    )(far(keep), far(got), far(last), *more)


def swap(value, axis, mask):
    size = lax.axis_size(axis)
    return lax.ppermute(value, axis, [(i, i ^ mask) for i in range(size)])


def bit_of(axis, mask):
    return jnp.where((lax.axis_index(axis) & mask) > 0, 1, 0).astype(jnp.int32).reshape(1)


def bits_of(size):
    return [1 << i for i in range(size.bit_length() - 1)]


def on_device(
    tokens,
    norm_gains,
    norm_biases,
    w_qkv,
    w_attn_out,
    w_in,
    w_out,
    segment_ids,
    expert_ids,
    slots,
    cotangent,
):
    ORDER.clear()
    tok, dim = tokens.shape
    head_dim = dim // HEADS
    wide = lax.axis_size("wide")
    narrow = lax.axis_size("narrow")
    units = w_in.shape[2]
    me_wide = lax.axis_index("wide")
    me_narrow = lax.axis_index("narrow")
    capacity = tok * 9 // (8 * wide)
    w_in = w_in[0]
    w_out = w_out[0]
    zs = wide // 2
    slots_all = zs * capacity
    groups = [list(range(i, i + zs // 4)) for i in range(0, zs, zs // 4)]
    apart = capacity % 16 == 0

    def joinable(blocks):
        return blocks if apart else [jnp.concatenate(blocks, axis=0)]

    def by_position(pieces):
        return list(pieces) if apart else [q for p in pieces for q in jnp.split(p, p.shape[0] // (2 * capacity))]

    def piece_rows(group):
        return [2 * capacity] * len(group) if apart else [2 * capacity * len(group)]

    away = expert_ids ^ me_wide
    kept = slots < capacity
    base = (away >> 1) * capacity + slots
    core = away & 1
    nowhere = 2 * slots_all
    place_own = jnp.where(kept & (core == 0), base, nowhere).astype(jnp.int32)[None, :]
    place_sent = jnp.where(kept & (core == 1), base, nowhere).astype(jnp.int32)[None, :]
    places = [place_own, swap(place_sent, "wide", 1)]
    place_col = jnp.where(kept, core * slots_all + base, nowhere).astype(jnp.int32)[:, None]
    doc_col = segment_ids.reshape(tok, 1)

    def exchange(blocks, positions):
        return [swap(blocks[z], "wide", 2 * z) if z else blocks[z] for z in positions]

    def bring_back(blocks, cost=0):
        if not apart:
            theirs = jnp.concatenate([b[capacity:] for b in blocks], axis=0)
            own = [(jnp.concatenate([b[:capacity] for b in blocks], axis=0), slots_all)]
        else:
            theirs = second_halves(blocks, capacity, cost=cost)
            own = [(b, capacity) for b in blocks]
        return own + [(swap(theirs, "wide", 1), slots_all)]

    cotangent_other = swap(cotangent, "wide", 1)
    if apart:
        sent_grads = dispatch_side(places[0], far(cotangent), zs, capacity, 0)
        sent_grads = dispatch_side(places[1], cotangent_other, zs, capacity, 1, sent_grads)
    else:
        sent_grads = dispatch_rows(places, [cotangent, cotangent_other], zs, capacity)
    expert_grads = exchange(separate(sent_grads, zs, capacity), range(zs))
    normed = first_norm(tokens, norm_gains, norm_biases)

    projected = project(normed, w_qkv)
    mixed_heads, mixed_low, log_total = attn_fwd(projected, doc_col, head_dim)
    many = tok - LAST_ROWS
    middle_of = functools.partial(make_middle, tokens, mixed_heads, w_attn_out, norm_gains, norm_biases)
    middle, sent_first = middle_of(0, many)
    other_first = swap(sent_first, "wide", 1)
    gh = grad_hidden(joinable(expert_grads[: zs // 2]), w_out, 0, 2 * slots_all)
    middle, sent_last = middle_of(many, LAST_ROWS, [middle], after=expert_grads, cost=COST_MIDDLE)
    other_last = swap(sent_last, "wide", 1)
    sent_rows = dispatch_rows([p[:, :many] for p in places], [sent_first, other_first], zs, capacity)
    sent_rows = dispatch_rows([p[:, many:] for p in places], [sent_last, other_last], zs, capacity, sent_rows)
    expert_rows = exchange(separate(sent_rows, zs, capacity), range(zs))

    gh = grad_hidden(joinable(expert_grads[zs // 2 :]), w_out, slots_all, 2 * slots_all, [gh])
    grads_t = turned(joinable(expert_grads))
    held = ()
    back_grads = []
    for group in groups:
        blocks = joinable([expert_rows[z] for z in group])
        outs = expert(blocks, gh, w_in, 2 * group[0] * capacity, held, piece_rows(group))
        held = outs[:2]
        pieces = by_position(outs[2:])
        back_grads += exchange({z: pieces[i] for i, z in enumerate(group)}, group)
    hidden, grad_preact = held

    masks = [(1, 2), (2, 1)]
    sides = range(2)
    table = jnp.array([3, 1, 2, 0], jnp.int32) ^ me_narrow

    def first_step(send):
        return [swap(send[side], "narrow", masks[side][0]) for side in sides]

    send_a, send_b, *keep_out = weight_parts(grads_t, hidden, table, 3)
    got_out = first_step([send_a, send_b])
    keep_out = weight_parts(grads_t, hidden, table, 1, keep_out)
    produced = make_produced(hidden, w_out, piece_rows(range(zs)))
    back_rows = exchange(by_position(produced), range(zs))
    rows_t = turned(joinable(expert_rows))
    send_a, send_b, *keep_in = weight_parts(rows_t, grad_preact, table)
    got_in = first_step([send_a, send_b])
    back_grads = bring_back(back_grads, COST_GATE)
    grad_middle, grad_attn_t, grad_heads, sums_two = second_back(
        place_col, middle, cotangent, back_grads, w_attn_out, norm_gains, after=got_out
    )
    attn = functools.partial(
        attn_bwd, projected, mixed_heads, mixed_low, grad_heads, log_total, doc_col, head_dim
    )
    pairs = dim // 128
    held = attn(0, PAIRS_FIRST)
    again = add_second(
        [pair for side in sides for pair in ((keep_out[side], got_out[side]), (keep_in[side], got_in[side]))]
    )
    last = [swap(again[side], "narrow", masks[side][1]) for side in sides]
    grads, grads_all_t = attn(PAIRS_FIRST, pairs - PAIRS_FIRST, held)
    back_rows = bring_back(back_rows)
    grads_all_t = grads_all_t.reshape(3 * dim, tok)

    owners = narrow * wide
    own_qkv = 3 * dim // owners
    n_bits = bits_of(narrow)
    w_bits = bits_of(wide)
    names = [("narrow", b) for b in reversed(n_bits)] + [("wide", b) for b in reversed(w_bits)]
    core_bit = ("wide", 1)
    near = ("wide", w_bits[1])
    orders = [[near, ("narrow", 1), ("narrow", 2)], [("narrow", 1), ("narrow", 2), near]]
    bits = {name: bit_of(*name) for name in names}
    kept_a, sent_a, kept_b, sent_b = joint(
        grads_all_t, grad_attn_t, normed, mixed_heads, bits[core_bit], owners
    )
    got_a, got_b = [swap(sent, *core_bit) for sent in (sent_a, sent_b)]
    state = [(kept_a, got_a, names[:-1]), (kept_b, got_b, names[:-1])]

    def one_step(number, after=()):
        steps = [orders[side][number] for side in sides]
        places_left = [state[side][2].index(steps[side]) for side in sides]
        sets = [
            ([state[side][:2]], bits[steps[side]], 1 << (len(state[side][2]) - 1 - places_left[side]))
            for side in sides
        ]
        got = [swap(sent, *steps[side]) for side, sent in enumerate(add_half(sets, 1, number < 2, after=after))]
        for side, kept in enumerate(add_half(sets, 0, number < 2, number == 0, cost=12)):
            left = list(state[side][2])
            left.remove(steps[side])
            state[side] = (kept, got[side], left)

    rounds = [("narrow", n_bits)] + [("wide", w_bits[i : i + 2]) for i in range(0, len(w_bits), 2)]

    def send_sums(number):
        axis, some = rounds[number]
        others = sorted({sum(c) for c in itertools.product(*[(0, b) for b in some])} - {0})
        return [swap(sums, axis, m) for m in others]

    mixed = make_mixed(place_col, middle, back_rows, cost=9)
    one_step(0, last)
    d_tokens, sums_one = first_back(tokens, grad_middle, grads, w_qkv, norm_gains)
    one_step(1)
    sums = stack_sums(sums_one, sums_two)
    sums_got = send_sums(0)
    d_w_out = finish(keep_out[0], got_out[0], last[0], 0, True, 0)
    d_w_out = finish(keep_out[1], got_out[1], last[1], 0, True, 1, d_w_out)
    sums = add_rows([sums, *sums_got])
    one_step(2)
    sums_got = send_sums(1)
    d_w_in = finish(keep_in[0], got_in[0], last[0], 1, False, 0)
    d_w_in = finish(keep_in[1], got_in[1], last[1], 1, False, 1, d_w_in)
    sums = add_rows([sums, *sums_got])
    pairs = [state[side][:2] for side in sides]
    left = state[0][2]
    for number, step in enumerate((("wide", b) for b in w_bits[2:]), 2):
        at = left.index(step)
        sets = [(pairs, bits[step], 1 << (len(left) - 1 - at))]
        got = swap(add_half(sets, 1)[0], *step)
        pairs = [(add_half(sets, 0)[0], got)]
        left = left[:at] + left[at + 1 :]
        sums_got = send_sums(number) if number < len(rounds) else []
        sums = add_rows([sums, *sums_got])
    value = pairs[0][0][0].astype(F32) + pairs[0][1][0].astype(F32)
    d_w_qkv = value[:own_qkv].T
    d_w_attn_out = value[own_qkv:].T
    own = dim // owners
    sums = lax.dynamic_slice_in_dim(sums, (me_narrow * wide + me_wide) * own, own, 1)
    return (mixed, d_tokens, sums[:2], sums[2:], d_w_qkv, d_w_attn_out, d_w_in[None], d_w_out[None])


def solution(mesh):
    placed = (
        P(("narrow", "wide"), None),
        P(),
        P(),
        P(),
        P(),
        P("wide", None, None),
        P("wide", None, None),
        P(("narrow", "wide"), None),
        P(("narrow", "wide")),
        P(("narrow", "wide")),
        P(("narrow", "wide"), None),
    )
    return jax.shard_map(
        on_device,
        mesh=mesh,
        in_specs=placed,
        out_specs=(
            P(("narrow", "wide"), None),
            P(("narrow", "wide"), None),
            P(None, ("narrow", "wide")),
            P(None, ("narrow", "wide")),
            P(None, ("narrow", "wide")),
            P(None, ("narrow", "wide")),
            P("wide", None, "narrow"),
            P("wide", "narrow", None),
        ),
        check_vma=False,
    )
```

profile of v0, /device:TPU:0, one launch (start us, length us, event | category | flops | bytes accessed | tf_op | source)
XLA Modules:
  0.0 371.5 jit_solution(6899485116448335228)
XLA Ops:
  1.9 3.9 %shard_map.179 = (bf16[288,1024]{1,0:T(8,128)(2,1)}, bf16[288,1024]{1,0:T(8,128)(2,1)}, bf16[288,1024]{1,0:T(8,128)(2,1)}, bf16[288,1024]{1,0:T(8,128)(2,1)}, f32[8,128]{1,0:T(8,128)S(1)}) custom-call(s32[1,1024]{1,0:T(1,128)S(1)} %bitcast.69, bf16[1024,1024]{1,0:T(8,128)(2,1)} %refs_2_.7), custom_call_target="tpu_custom_call" | custom-call | flops 1 | tf_op jit(solution)/shard_map/pallas_call | solution.py:74
  5.8 2.3 shard_map.180
  8.1 3.0 collective-permute-start.2
  11.1 2.6 collective-permute-start.3
  13.9 4.7 %shard_map.181 = (bf16[1024,1024]{1,0:T(8,128)(2,1)}, f32[8,128]{1,0:T(8,128)S(1)}) custom-call(bf16[1024,1024]{1,0:T(8,128)(2,1)} %refs_0_.7, f32[2,1024]{1,0:T(2,128)} %refs_4_.7, f32[2,1024]{1,0:T(2,128)} %refs_4_.5, f32[8,128]{1,0:T(8,128)S(1)} %get-tuple-element.154.refs_3_), custom_call_target="tpu_custom_call" | custom-call | flops 1 | tf_op jit(solution)/shard_map/pallas_call | solution.py:74
  18.6 10.7 %shard_map.182 = (bf16[1024,3072]{1,0:T(8,128)(2,1)}, f32[8,128]{1,0:T(8,128)S(1)}) custom-call(bf16[1024,1024]{1,0:T(8,128)(2,1)} %get-tuple-element.155.refs_0_.refs_3_, bf16[1024,3072]{1,0:T(8,128)(2,1)} %refs_3_.7, f32[8,128]{1,0:T(8,128)S(1)} %get-tuple-element.156.refs_2_), custom_call_target="tpu_custom_call" | custom-call | flops 1 | tf_op jit(solution)/shard_map/pallas_call | solution.py:74
  29.3 18.5 %shard_map.183 = (bf16[1024,1024]{1,0:T(8,128)(2,1)S(1)}, bf16[1024,1024]{1,0:T(8,128)(2,1)}, f32[8,2,1024]{2,1,0:T(2,128)}, f32[8,128]{1,0:T(8,128)S(1)}) custom-call(s32[1024,1]{1,0:T(8,128)S(1)} %copy.38.refs_0_, bf16[1024,3072]{1,0:T(8,128)(2,1)} %get-tuple-element.157.refs_1_.refs_2_.refs_3_, ...), custom_call_target="tpu_custom_call" | custom-call | flops 1 | tf_op jit(solution)/shard_map/pallas_call | solution.py:74
  47.8 7.2 %shard_map.184 = (f32[1024,1024]{1,0:T(8,128)}, bf16[896,1024]{1,0:T(8,128)(2,1)S(1)}, f32[8,128]{1,0:T(8,128)S(1)}) custom-call(bf16[1024,1024]{1,0:T(8,128)(2,1)} %refs_0_.7, bf16[1024,1024]{1,0:T(8,128)(2,1)S(1)} %get-tuple-element.159.refs_1_.refs_4_, bf16[1024,1024]{1,0:T(8,128)(2,1)} %refs_3_.6, f32[2,1024]{1,0:T(2,128)} %refs_4_.7, ...), custom_call_target="tpu_custom_call" | custom-call | flops 1 | tf_op jit(solution)/shard_map/pallas_call | solution.py:74
  55.0 9.4 %shard_map.185 = (bf16[1152,4096]{1,0:T(8,128)(2,1)}, f32[8,128]{1,0:T(8,128)S(1)}) custom-call(bf16[4096,1024]{1,0:T(8,128)(2,1)} %bitcast.83, bf16[288,1024]{1,0:T(8,128)(2,1)S(1)} %copy-done.1, bf16[288,1024]{1,0:T(8,128)(2,1)S(1)} %collective-permute-done.2.refs_2_.refs_7_.refs_1_, f32[8,128]{1,0:T(8,128)S(1)} %get-tuple-element.166.refs_3_), custom_call_target="tpu_custom_call" | custom-call | flops 1 | tf_op jit(solution)/shard_map/pallas_call | solution.py:74
  64.4 2.9 shard_map.186
  67.8 2.6 shard_map.187
  71.2 1.0 collective-permute-start.9
  72.2 3.4 collective-permute-start.8
  75.6 9.5 %shard_map.189 = (bf16[1152,4096]{1,0:T(8,128)(2,1)}, f32[8,128]{1,0:T(8,128)S(1)}) custom-call(bf16[4096,1024]{1,0:T(8,128)(2,1)} %bitcast.84, bf16[288,1024]{1,0:T(8,128)(2,1)} %collective-permute-done.3.refs_8_.refs_1_.refs_2_, bf16[288,1024]{1,0:T(8,128)(2,1)} %collective-permute-done.4.refs_9_.refs_2_.refs_3_, ...), custom_call_target="tpu_custom_call", output_to_operand_aliasing={{0}: (3, {})} | custom-call | flops 1 | tf_op jit(solution)/shard_map/pallas_call | solution.py:74
  85.2 3.3 shard_map.190
  88.5 12.0 %shard_map.191 = (bf16[1152,4096]{1,0:T(8,128)(2,1)}, bf16[1152,4096]{1,0:T(8,128)(2,1)}, bf16[288,1024]{1,0:T(8,128)(2,1)}, f32[8,128]{1,0:T(8,128)S(1)}) custom-call(bf16[1024,4096]{1,0:T(8,128)(2,1)} %bitcast.79, bf16[1152,4096]{1,0:T(8,128)(2,1)} %get-tuple-element.179.refs_1_, bf16[288,1024]{1,0:T(8,128)(2,1)S(1)} %get-tuple-element.183.refs_2_.refs_0_, ...), custom_call_target="tpu_custom_call" | custom-call | flops 1 | tf_op jit(solution)/shard_map/pallas_call | solution.py:74
  100.4 11.8 %shard_map.192 = (bf16[1152,4096]{1,0:T(8,128)(2,1)}, bf16[1152,4096]{1,0:T(8,128)(2,1)}, bf16[288,1024]{1,0:T(8,128)(2,1)}, f32[8,128]{1,0:T(8,128)S(1)}) custom-call(bf16[1024,4096]{1,0:T(8,128)(2,1)} %bitcast.80, bf16[1152,4096]{1,0:T(8,128)(2,1)} %get-tuple-element.179.refs_1_, ...), custom_call_target="tpu_custom_call", output_to_operand_aliasing={{0}: (3, {}), {1}: (4, {})} | custom-call | flops 1 | tf_op jit(solution)/shard_map/pallas_call | solution.py:74
  112.8 2.3 collective-permute-done.8.refs_2_
  115.1 11.7 %shard_map.193 = (bf16[1152,4096]{1,0:T(8,128)(2,1)}, bf16[1152,4096]{1,0:T(8,128)(2,1)}, bf16[288,1024]{1,0:T(8,128)(2,1)}, f32[8,128]{1,0:T(8,128)S(1)}) custom-call(bf16[1024,4096]{1,0:T(8,128)(2,1)} %bitcast.81, bf16[1152,4096]{1,0:T(8,128)(2,1)} %get-tuple-element.179.refs_1_, ...), custom_call_target="tpu_custom_call", output_to_operand_aliasing={{0}: (3, {}), {1}: (4, {})} | custom-call | flops 1 | tf_op jit(solution)/shard_map/pallas_call | solution.py:74
  126.8 1.7 collective-permute-start.14
  128.5 12.4 %shard_map.194 = (bf16[1152,4096]{1,0:T(8,128)(2,1)}, bf16[1152,4096]{1,0:T(8,128)(2,1)}, bf16[288,1024]{1,0:T(8,128)(2,1)}, f32[8,128]{1,0:T(8,128)S(1)}) custom-call(bf16[1024,4096]{1,0:T(8,128)(2,1)} %bitcast.82, bf16[1152,4096]{1,0:T(8,128)(2,1)} %get-tuple-element.179.refs_1_, ...), custom_call_target="tpu_custom_call", output_to_operand_aliasing={{0}: (3, {}), {1}: (4, {})} | custom-call | flops 1 | tf_op jit(solution)/shard_map/pallas_call | solution.py:74
  140.9 1.0 collective-permute-start.15
  141.8 13.8 %shard_map.195 = (bf16[2,512,1024]{2,1,0:T(8,128)(2,1)}, bf16[2,512,1024]{2,1,0:T(8,128)(2,1)}, bf16[2,512,1024]{2,1,0:T(8,128)(2,1)}, bf16[2,512,1024]{2,1,0:T(8,128)(2,1)}, f32[8,128]{1,0:T(8,128)S(1)}) custom-call(s32[4]{0:T(128)S(1)} %broadcast_xor_fusion.refs_0_, bf16[1024,1152]{1,0:T(8,128)(2,1)} %get-tuple-element.196.refs_1_, ...), custom_call_target="tpu_custom_call" | custom-call | flops 1 | tf_op jit(solution)/shard_map/pallas_call | solution.py:74
  155.7 1.5 collective-permute-start.17
  157.2 1.5 collective-permute-start.18
  158.7 6.8 %shard_map.196 = (bf16[2,512,1024]{2,1,0:T(8,128)(2,1)}, bf16[2,512,1024]{2,1,0:T(8,128)(2,1)}, f32[8,128]{1,0:T(8,128)S(1)}) custom-call(s32[4]{0:T(128)S(1)} %broadcast_xor_fusion.refs_0_, bf16[1024,1152]{1,0:T(8,128)(2,1)} %get-tuple-element.196.refs_1_, ...), custom_call_target="tpu_custom_call", output_to_operand_aliasing={{0}: (3, {}), {1}: (4, {})} | custom-call | flops 1 | tf_op jit(solution)/shard_map/pallas_call | solution.py:74
  165.5 16.1 %shard_map.197 = (bf16[288,1024]{1,0:T(8,128)(2,1)S(1)}, bf16[288,1024]{1,0:T(8,128)(2,1)}, bf16[288,1024]{1,0:T(8,128)(2,1)}, bf16[288,1024]{1,0:T(8,128)(2,1)}, f32[8,128]{1,0:T(8,128)S(1)}) custom-call(bf16[1152,4096]{1,0:T(8,128)(2,1)} %get-tuple-element.195.refs_2_.refs_0_, bf16[4096,1024]{1,0:T(8,128)(2,1)} %bitcast.85, ...), custom_call_target="tpu_custom_call" | custom-call | flops 1 | tf_op jit(solution)/shard_map/pallas_call | solution.py:74
  181.6 2.1 shard_map.198
  183.7 16.7 %shard_map.199 = (bf16[2,512,1024]{2,1,0:T(8,128)(2,1)}, bf16[2,512,1024]{2,1,0:T(8,128)(2,1)}, bf16[2,512,1024]{2,1,0:T(8,128)(2,1)}, bf16[2,512,1024]{2,1,0:T(8,128)(2,1)}, f32[8,128]{1,0:T(8,128)S(1)}) custom-call(s32[4]{0:T(128)S(1)} %broadcast_xor_fusion.refs_0_, bf16[1024,1152]{1,0:T(8,128)(2,1)} %get-tuple-element.212.refs_1_, ...), custom_call_target="tpu_custom_call" | custom-call | flops 1 | tf_op jit(solution)/shard_map/pallas_call | solution.py:74
  201.5 1.2 shard_map.200
  202.8 2.8 collective-permute-done.16.refs_9_
  205.6 1.0 collective-permute-start.10
  206.6 2.5 collective-permute-start.11
  210.7 12.6 %shard_map.201 = (f32[1024,1024]{1,0:T(8,128)}, bf16[1024,1024]{1,0:T(8,128)(2,1)}, bf16[1024,1024]{1,0:T(8,128)(2,1)}, f32[2,1024]{1,0:T(2,128)S(1)}, f32[8,128]{1,0:T(8,128)S(1)}) custom-call(s32[1024,1]{1,0:T(8,128)S(1)} %copy.42.refs_0_, f32[1024,1024]{1,0:T(8,128)} %get-tuple-element.168.refs_1_, bf16[1024,1024]{1,0:T(8,128)(2,1)} %refs_2_.7, ...), custom_call_target="tpu_custom_call" | custom-call | flops 1 | tf_op jit(solution)/shard_map/pallas_call | solution.py:74
  223.3 22.2 %shard_map.202 = (bf16[3,1024,1024]{2,1,0:T(8,128)(2,1)}, bf16[3,1024,1024]{2,1,0:T(8,128)(2,1)}, f32[8,128]{1,0:T(8,128)S(1)}) custom-call(s32[1024,1]{1,0:T(8,128)S(1)} %copy.38.refs_0_, bf16[1024,3072]{1,0:T(8,128)(2,1)} %get-tuple-element.157.refs_1_.refs_2_.refs_3_, bf16[1024,3072]{1,0:T(8,128)(2,1)} %get-tuple-element.157.refs_1_.refs_2_.refs_3_, ...), custom_call_target="tpu_custom_call" | custom-call | flops 1 | tf_op jit(solution)/shard_map/pallas_call | solution.py:74
  246.4 1.2 collective-permute-done.20.refs_7_.refs_1_
  247.6 5.3 %shard_map.203 = (bf16[2,544,1024]{2,1,0:T(8,128)(2,1)}, bf16[2,544,1024]{2,1,0:T(8,128)(2,1)}, f32[8,128]{1,0:T(8,128)S(1)}) custom-call(bf16[2,512,1024]{2,1,0:T(8,128)(2,1)} %get-tuple-element.225.refs_0_, bf16[2,512,1024]{2,1,0:T(8,128)(2,1)} %copy-done.13, bf16[2,512,1024]{2,1,0:T(8,128)(2,1)} %get-tuple-element.226.refs_2_.refs_0_, ...), custom_call_target="tpu_custom_call" | custom-call | flops 1 | tf_op jit(solution)/shard_map/pallas_call | solution.py:74
  252.8 1.5 collective-permute-start.24
  254.9 14.4 %shard_map.204 = (bf16[3,1024,1024]{2,1,0:T(8,128)(2,1)}, bf16[3,1024,1024]{2,1,0:T(8,128)(2,1)}, f32[8,128]{1,0:T(8,128)S(1)}) custom-call(s32[1024,1]{1,0:T(8,128)S(1)} %copy.38.refs_0_, bf16[1024,3072]{1,0:T(8,128)(2,1)} %get-tuple-element.157.refs_1_.refs_2_.refs_3_, ...), custom_call_target="tpu_custom_call", output_to_operand_aliasing={{0}: (8, {}), {1}: (9, {})} | custom-call | flops 1 | tf_op jit(solution)/shard_map/pallas_call | solution.py:74
  269.4 2.3 shard_map.205
  271.7 13.4 %shard_map.206 = (bf16[16,128,512]{2,1,0:T(8,128)(2,1)}, bf16[16,128,512]{2,1,0:T(8,128)(2,1)}, bf16[16,128,512]{2,1,0:T(8,128)(2,1)}, bf16[16,128,512]{2,1,0:T(8,128)(2,1)}, f32[8,128]{1,0:T(8,128)S(1)}) custom-call(s32[1]{0:T(128)} %bitcast.6.refs_0_, bf16[3072,1024]{1,0:T(8,128)(2,1)} %bitcast.86, bf16[1024,1024]{1,0:T(8,128)(2,1)} %get-tuple-element.236.refs_2_, ...), custom_call_target="tpu_custom_call" | custom-call | flops 1 | tf_op jit(solution)/shard_map/pallas_call | solution.py:74
  285.7 7.2 %shard_map.207 = (bf16[1024,1024]{1,0:T(8,128)(2,1)}, f32[8,128]{1,0:T(8,128)S(1)}) custom-call(s32[1024,1]{1,0:T(8,128)S(1)} %copy.42.refs_0_, f32[1024,1024]{1,0:T(8,128)} %get-tuple-element.168.refs_1_, bf16[288,1024]{1,0:T(8,128)(2,1)} %copy-done.8, bf16[288,1024]{1,0:T(8,128)(2,1)} %copy-done.10, bf16[288,1024]{1,0:T(8,128)(2,1)} %copy-done.11, ...), custom_call_target="tpu_custom_call" | custom-call | flops 10350000128 | tf_op jit(solution)/shard_map/pallas_call | solution.py:74
  292.8 8.5 %collective-permute-done.24.refs_6_.refs_2_ = bf16[2,544,1024]{2,1,0:T(8,128)(2,1)} collective-permute-done((bf16[2,544,1024]{2,1,0:T(8,128)(2,1)}, bf16[2,544,1024]{2,1,0:T(8,128)(2,1)}, u32[]{:S(2)}, u32[]{:S(2)}) %collective-permute-start.24) | collective-permute-done | bytes 2228256 | tf_op jit(solution)/shard_map/ppermute | solution.py:986
  301.4 0.9 collective-permute-done.25.refs_7_.refs_2_
  302.3 2.1 shard_map.208
  305.0 1.5 collective-permute-start.27
  306.5 3.3 shard_map.209
  309.7 14.2 %shard_map.210 = (f32[1024,1024]{1,0:T(8,128)}, f32[2,1024]{1,0:T(2,128)S(1)}, f32[8,128]{1,0:T(8,128)S(1)}) custom-call(bf16[1024,1024]{1,0:T(8,128)(2,1)} %refs_0_.7, f32[1024,1024]{1,0:T(8,128)} %get-tuple-element.240.refs_1_, bf16[3,1024,1024]{2,1,0:T(8,128)(2,1)} %get-tuple-element.241.refs_2_, bf16[1024,3072]{1,0:T(8,128)(2,1)} %refs_3_.7, ...), custom_call_target="tpu_custom_call" | custom-call | flops 1 | tf_op jit(solution)/shard_map/pallas_call | solution.py:74
  324.0 1.9 collective-permute-done.26
  326.7 1.4 shard_map.211
  328.2 1.8 collective-permute-start.34
  330.5 1.4 shard_map.212
  332.4 1.4 collective-permute-start.29
  333.8 1.7 collective-permute-start.30
  335.5 3.2 shard_map.214
  338.7 3.2 shard_map.215
  342.0 1.7 collective-permute-start.32
  344.0 1.5 collective-permute-start.37
  345.5 1.6 collective-permute-start.38
  347.2 3.0 shard_map.219
  350.3 3.0 shard_map.220
  353.3 2.0 collective-permute-start.36
  355.4 1.7 collective-permute-start.39
  359.3 10.5 %collective-permute-done.39 = bf16[1,128,1024]{2,1,0:T(8,128)(2,1)S(1)} collective-permute-done((bf16[1,128,1024]{2,1,0:T(8,128)(2,1)S(1)}, bf16[1,128,1024]{2,1,0:T(8,128)(2,1)S(1)}, u32[]{:S(2)}, u32[]{:S(2)}) %collective-permute-start.39) | collective-permute-done | bytes 262176 | tf_op jit(solution)/shard_map/ppermute | solution.py:986
  (109 shorter events, 14.9 us)
Async XLA Ops:
  0.6 5.2 %collective-permute-start.1 = (bf16[1024,1024]{1,0:T(8,128)(2,1)}, bf16[1024,1024]{1,0:T(8,128)(2,1)S(1)}, u32[]{:S(2)}, u32[]{:S(2)}) collective-permute-start(bf16[1024,1024]{1,0:T(8,128)(2,1)} %refs_2_.7), channel_id=1, source_target_pairs={{0,1},{1,0},{2,3},{3,2},{4,5},{5,4},{6,7},{7,6},{8,9},{9,8},{10,11... | collective-permute-start | bytes 6291464 | tf_op jit(solution)/shard_map/ppermute | solution.py:986
  1.9 3.9 %collective-permute-start = (s32[1,1024]{1,0:T(1,128)S(1)}, s32[1,1024]{1,0:T(1,128)S(1)}, u32[]{:S(2)}, u32[]{:S(2)}) collective-permute-start(s32[1,1024]{1,0:T(1,128)S(1)} %bitcast.99), channel_id=1, source_target_pairs={{0,1},{1,0},{2,3},{3,2},{4,5},{5,4},{6,7},{7,6},{8,9},{9,8},{10,11... | collective-permute-start | bytes 12296 | tf_op jit(solution)/shard_map/ppermute | solution.py:986
  5.8 7.9 %copy-start.15 = (s32[1,1024]{1,0:T(1,128)S(1)}, s32[1,1024]{1,0:T(1,128)}, u32[]{:S(2)}) copy-start(s32[1,1024]{1,0:T(1,128)} %param.19) | copy-start | bytes 12292
  8.1 46.8 %collective-permute-start.2 = (bf16[288,1024]{1,0:T(8,128)(2,1)}, bf16[288,1024]{1,0:T(8,128)(2,1)S(1)}, u32[]{:S(2)}, u32[]{:S(2)}) collective-permute-start(bf16[288,1024]{1,0:T(8,128)(2,1)} %get-tuple-element.163), channel_id=1, source_target_pairs={{0,2},{1,3},{2,0},{3,1},{4,6},{5,7},{6,4},{7,5},{8,10},{9,11},{10,... | collective-permute-start | bytes 1769480 | tf_op jit(solution)/shard_map/ppermute | solution.py:986
  11.1 53.3 %collective-permute-start.3 = (bf16[288,1024]{1,0:T(8,128)(2,1)}, bf16[288,1024]{1,0:T(8,128)(2,1)}, u32[]{:S(2)}, u32[]{:S(2)}) collective-permute-start(bf16[288,1024]{1,0:T(8,128)(2,1)} %get-tuple-element.164), channel_id=1, source_target_pairs={{0,4},{1,5},{2,6},{3,7},{4,0},{5,1},{6,2},{7,3},{8,12},{9,13},{10,... | collective-permute-start | bytes 1769480 | tf_op jit(solution)/shard_map/ppermute | solution.py:986
  13.7 50.7 %collective-permute-start.4 = (bf16[288,1024]{1,0:T(8,128)(2,1)}, bf16[288,1024]{1,0:T(8,128)(2,1)}, u32[]{:S(2)}, u32[]{:S(2)}) collective-permute-start(bf16[288,1024]{1,0:T(8,128)(2,1)} %get-tuple-element.165), channel_id=1, source_target_pairs={{0,6},{1,7},{2,4},{3,5},{4,2},{5,3},{6,0},{7,1},{8,14},{9,15},{10,... | collective-permute-start | bytes 1769480 | tf_op jit(solution)/shard_map/ppermute | solution.py:986
  47.8 16.6 %copy-start = (bf16[1024,1024]{1,0:T(8,128)(2,1)}, bf16[1024,1024]{1,0:T(8,128)(2,1)S(1)}, u32[]{:S(2)}) copy-start(bf16[1024,1024]{1,0:T(8,128)(2,1)S(1)} %get-tuple-element.159.refs_1_.refs_4_) | copy-start | bytes 6291460
  47.8 7.2 %copy-start.1 = (bf16[288,1024]{1,0:T(8,128)(2,1)S(1)}, bf16[288,1024]{1,0:T(8,128)(2,1)}, u32[]{:S(2)}) copy-start(bf16[288,1024]{1,0:T(8,128)(2,1)} %get-tuple-element.162.refs_1_.refs_6_.refs_0_) | copy-start | bytes 1769476
  54.9 12.8 %collective-permute-start.6 = (bf16[896,1024]{1,0:T(8,128)(2,1)S(1)}, bf16[896,1024]{1,0:T(8,128)(2,1)S(1)}, u32[]{:S(2)}, u32[]{:S(2)}) collective-permute-start(bf16[896,1024]{1,0:T(8,128)(2,1)S(1)} %get-tuple-element.171.refs_2_), channel_id=1, source_target_pairs={{0,1},{1,0},{2,3},{3,2},{4,5},{5,4},{6,7},{7,6},{8,9},{9,8},{10,11... | collective-permute-start | bytes 5505032 | tf_op jit(solution)/shard_map/ppermute | solution.py:986
  54.9 9.4 %copy-start.3 = (bf16[288,1024]{1,0:T(8,128)(2,1)}, bf16[288,1024]{1,0:T(8,128)(2,1)S(1)}, u32[]{:S(2)}) copy-start(bf16[288,1024]{1,0:T(8,128)(2,1)S(1)} %collective-permute-done.2.refs_2_.refs_7_.refs_1_) | copy-start | bytes 1769476
  67.2 3.1 collective-permute-start.5
  71.2 29.3 %collective-permute-start.9 = (bf16[288,1024]{1,0:T(8,128)(2,1)S(1)}, bf16[288,1024]{1,0:T(8,128)(2,1)S(1)}, u32[]{:S(2)}, u32[]{:S(2)}) collective-permute-start(bf16[288,1024]{1,0:T(8,128)(2,1)S(1)} %get-tuple-element.182), channel_id=1, source_target_pairs={{0,2},{1,3},{2,0},{3,1},{4,6},{5,7},{6,4},{7,5},{8,10},{9,11},{10,... | collective-permute-start | bytes 1769480 | tf_op jit(solution)/shard_map/ppermute | solution.py:986
  72.2 42.9 %collective-permute-start.8 = (bf16[288,1024]{1,0:T(8,128)(2,1)S(1)}, bf16[288,1024]{1,0:T(8,128)(2,1)S(1)}, u32[]{:S(2)}, u32[]{:S(2)}) collective-permute-start(bf16[288,1024]{1,0:T(8,128)(2,1)S(1)} %get-tuple-element.181), channel_id=1, source_target_pairs={{0,4},{1,5},{2,6},{3,7},{4,0},{5,1},{6,2},{7,3},{8,12},{9,13},{10,... | collective-permute-start | bytes 1769480 | tf_op jit(solution)/shard_map/ppermute | solution.py:986
  75.6 52.9 %collective-permute-start.7 = (bf16[288,1024]{1,0:T(8,128)(2,1)S(1)}, bf16[288,1024]{1,0:T(8,128)(2,1)S(1)}, u32[]{:S(2)}, u32[]{:S(2)}) collective-permute-start(bf16[288,1024]{1,0:T(8,128)(2,1)S(1)} %get-tuple-element.180), channel_id=1, source_target_pairs={{0,6},{1,7},{2,4},{3,5},{4,2},{5,3},{6,0},{7,1},{8,14},{9,15},{10,... | collective-permute-start | bytes 1769480 | tf_op jit(solution)/shard_map/ppermute | solution.py:986
  75.6 9.5 %copy-start.2 = (bf16[288,1024]{1,0:T(8,128)(2,1)S(1)}, bf16[288,1024]{1,0:T(8,128)(2,1)}, u32[]{:S(2)}) copy-start(bf16[288,1024]{1,0:T(8,128)(2,1)} %get-tuple-element.162.refs_1_.refs_6_.refs_0_) | copy-start | bytes 1769476
  75.6 9.5 %copy-start.4 = (bf16[288,1024]{1,0:T(8,128)(2,1)S(1)}, bf16[288,1024]{1,0:T(8,128)(2,1)}, u32[]{:S(2)}) copy-start(bf16[288,1024]{1,0:T(8,128)(2,1)} %copy-done.3) | copy-start | bytes 1769476
  112.2 88.2 %collective-permute-start.13 = (bf16[288,1024]{1,0:T(8,128)(2,1)}, bf16[288,1024]{1,0:T(8,128)(2,1)}, u32[]{:S(2)}, u32[]{:S(2)}) collective-permute-start(bf16[288,1024]{1,0:T(8,128)(2,1)} %get-tuple-element.208), channel_id=1, source_target_pairs={{0,2},{1,3},{2,0},{3,1},{4,6},{5,7},{6,4},{7,5},{8,10},{9,11},{10,... | collective-permute-start | bytes 1769480 | tf_op jit(solution)/shard_map/ppermute | solution.py:986
  126.8 74.1 %collective-permute-start.14 = (bf16[288,1024]{1,0:T(8,128)(2,1)}, bf16[288,1024]{1,0:T(8,128)(2,1)}, u32[]{:S(2)}, u32[]{:S(2)}) collective-permute-start(bf16[288,1024]{1,0:T(8,128)(2,1)} %get-tuple-element.209), channel_id=1, source_target_pairs={{0,4},{1,5},{2,6},{3,7},{4,0},{5,1},{6,2},{7,3},{8,12},{9,13},{10,... | collective-permute-start | bytes 1769480 | tf_op jit(solution)/shard_map/ppermute | solution.py:986
  128.5 12.4 %copy-start.5 = (bf16[288,1024]{1,0:T(8,128)(2,1)}, bf16[288,1024]{1,0:T(8,128)(2,1)S(1)}, u32[]{:S(2)}) copy-start(bf16[288,1024]{1,0:T(8,128)(2,1)S(1)} %collective-permute-done.7.refs_2_.refs_3_) | copy-start | bytes 1769476
  128.5 13.3 %copy-start.16 = (s32[4]{0:T(128)S(1)}, s32[4]{0:T(128)}, u32[]{:S(2)}) copy-start(s32[4]{0:T(128)} %constant.32.clone) | copy-start | bytes 52
  140.9 60.6 %collective-permute-start.15 = (bf16[288,1024]{1,0:T(8,128)(2,1)}, bf16[288,1024]{1,0:T(8,128)(2,1)}, u32[]{:S(2)}, u32[]{:S(2)}) collective-permute-start(bf16[288,1024]{1,0:T(8,128)(2,1)} %get-tuple-element.210), channel_id=1, source_target_pairs={{0,6},{1,7},{2,4},{3,5},{4,2},{5,3},{6,0},{7,1},{8,14},{9,15},{10,... | collective-permute-start | bytes 1769480 | tf_op jit(solution)/shard_map/ppermute | solution.py:986
  155.7 50.9 %collective-permute-start.17 = (bf16[2,512,1024]{2,1,0:T(8,128)(2,1)}, bf16[2,512,1024]{2,1,0:T(8,128)(2,1)S(1)}, u32[]{:S(2)}, u32[]{:S(2)}) collective-permute-start(bf16[2,512,1024]{2,1,0:T(8,128)(2,1)} %get-tuple-element.217), channel_id=1, source_target_pairs={{0,8},{8,0},{16,24},{24,16},{1,9},{9,1},{17,25},{25,17},{2,10},{10... | collective-permute-start | bytes 6291464 | tf_op jit(solution)/shard_map/ppermute | solution.py:986
  157.2 52.0 %collective-permute-start.18 = (bf16[2,512,1024]{2,1,0:T(8,128)(2,1)}, bf16[2,512,1024]{2,1,0:T(8,128)(2,1)S(1)}, u32[]{:S(2)}, u32[]{:S(2)}) collective-permute-start(bf16[2,512,1024]{2,1,0:T(8,128)(2,1)} %get-tuple-element.218), channel_id=1, source_target_pairs={{0,16},{8,24},{16,0},{24,8},{1,17},{9,25},{17,1},{25,9},{2,18},{10... | collective-permute-start | bytes 6291464 | tf_op jit(solution)/shard_map/ppermute | solution.py:986
  165.5 16.2 %copy-start.6 = (bf16[288,1024]{1,0:T(8,128)(2,1)S(1)}, bf16[288,1024]{1,0:T(8,128)(2,1)}, u32[]{:S(2)}) copy-start(bf16[288,1024]{1,0:T(8,128)(2,1)} %copy-done.5) | copy-start | bytes 1769476
  181.6 2.1 copy-start.8
  183.7 17.8 %copy-start.7 = (bf16[288,1024]{1,0:T(8,128)(2,1)S(1)}, bf16[288,1024]{1,0:T(8,128)(2,1)}, u32[]{:S(2)}) copy-start(bf16[288,1024]{1,0:T(8,128)(2,1)} %get-tuple-element.207.refs_0_.refs_5_) | copy-start | bytes 1769476
  200.4 45.9 %collective-permute-start.19 = (bf16[2,512,1024]{2,1,0:T(8,128)(2,1)}, bf16[2,512,1024]{2,1,0:T(8,128)(2,1)}, u32[]{:S(2)}, u32[]{:S(2)}) collective-permute-start(bf16[2,512,1024]{2,1,0:T(8,128)(2,1)} %get-tuple-element.227), channel_id=1, source_target_pairs={{0,8},{8,0},{16,24},{24,16},{1,9},{9,1},{17,25},{25,17},{2,10},{10... | collective-permute-start | bytes 6291464 | tf_op jit(solution)/shard_map/ppermute | solution.py:986
  201.0 46.6 %collective-permute-start.20 = (bf16[2,512,1024]{2,1,0:T(8,128)(2,1)}, bf16[2,512,1024]{2,1,0:T(8,128)(2,1)}, u32[]{:S(2)}, u32[]{:S(2)}) collective-permute-start(bf16[2,512,1024]{2,1,0:T(8,128)(2,1)} %get-tuple-element.230), channel_id=1, source_target_pairs={{0,16},{8,24},{16,0},{24,8},{1,17},{9,25},{17,1},{25,9},{2,18},{10... | collective-permute-start | bytes 6291464 | tf_op jit(solution)/shard_map/ppermute | solution.py:986
  202.7 2.9 collective-permute-start.16
  205.6 4.4 %copy-start.14 = (bf16[576,1024]{1,0:T(8,128)(2,1)}, bf16[576,1024]{1,0:T(8,128)(2,1)S(1)}, u32[]{:S(2)}) copy-start(bf16[576,1024]{1,0:T(8,128)(2,1)S(1)} %collective-permute-done.16.refs_9_) | copy-start | bytes 3538948
  205.6 63.7 %collective-permute-start.10 = (bf16[288,1024]{1,0:T(8,128)(2,1)}, bf16[288,1024]{1,0:T(8,128)(2,1)S(1)}, u32[]{:S(2)}, u32[]{:S(2)}) collective-permute-start(bf16[288,1024]{1,0:T(8,128)(2,1)} %get-tuple-element.203), channel_id=1, source_target_pairs={{0,2},{1,3},{2,0},{3,1},{4,6},{5,7},{6,4},{7,5},{8,10},{9,11},{10,... | collective-permute-start | bytes 1769480 | tf_op jit(solution)/shard_map/ppermute | solution.py:986
  206.6 3.4 copy-start.13
  206.6 62.8 %collective-permute-start.11 = (bf16[288,1024]{1,0:T(8,128)(2,1)}, bf16[288,1024]{1,0:T(8,128)(2,1)S(1)}, u32[]{:S(2)}, u32[]{:S(2)}) collective-permute-start(bf16[288,1024]{1,0:T(8,128)(2,1)} %get-tuple-element.204), channel_id=1, source_target_pairs={{0,4},{1,5},{2,6},{3,7},{4,0},{5,1},{6,2},{7,3},{8,12},{9,13},{10,... | collective-permute-start | bytes 1769480 | tf_op jit(solution)/shard_map/ppermute | solution.py:986
  209.1 1.3 copy-start.12
  209.1 60.3 %collective-permute-start.12 = (bf16[288,1024]{1,0:T(8,128)(2,1)}, bf16[288,1024]{1,0:T(8,128)(2,1)}, u32[]{:S(2)}, u32[]{:S(2)}) collective-permute-start(bf16[288,1024]{1,0:T(8,128)(2,1)} %get-tuple-element.205), channel_id=1, source_target_pairs={{0,6},{1,7},{2,4},{3,5},{4,2},{5,3},{6,0},{7,1},{8,14},{9,15},{10,... | collective-permute-start | bytes 1769480 | tf_op jit(solution)/shard_map/ppermute | solution.py:986
  252.8 48.5 %collective-permute-start.24 = (bf16[2,544,1024]{2,1,0:T(8,128)(2,1)}, bf16[2,544,1024]{2,1,0:T(8,128)(2,1)}, u32[]{:S(2)}, u32[]{:S(2)}) collective-permute-start(bf16[2,544,1024]{2,1,0:T(8,128)(2,1)} %get-tuple-element.246), channel_id=1, source_target_pairs={{0,16},{8,24},{16,0},{24,8},{1,17},{9,25},{17,1},{25,9},{2,18},{10... | collective-permute-start | bytes 6684680 | tf_op jit(solution)/shard_map/ppermute | solution.py:986
  254.4 47.9 %collective-permute-start.25 = (bf16[2,544,1024]{2,1,0:T(8,128)(2,1)}, bf16[2,544,1024]{2,1,0:T(8,128)(2,1)}, u32[]{:S(2)}, u32[]{:S(2)}) collective-permute-start(bf16[2,544,1024]{2,1,0:T(8,128)(2,1)} %get-tuple-element.247), channel_id=1, source_target_pairs={{0,8},{8,0},{16,24},{24,16},{1,9},{9,1},{17,25},{25,17},{2,10},{10... | collective-permute-start | bytes 6684680 | tf_op jit(solution)/shard_map/ppermute | solution.py:986
  254.9 14.5 %copy-start.9 = (bf16[288,1024]{1,0:T(8,128)(2,1)S(1)}, bf16[288,1024]{1,0:T(8,128)(2,1)}, u32[]{:S(2)}) copy-start(bf16[288,1024]{1,0:T(8,128)(2,1)} %copy-done.8) | copy-start | bytes 1769476
  269.4 15.7 %copy-start.10 = (bf16[288,1024]{1,0:T(8,128)(2,1)}, bf16[288,1024]{1,0:T(8,128)(2,1)S(1)}, u32[]{:S(2)}) copy-start(bf16[288,1024]{1,0:T(8,128)(2,1)S(1)} %collective-permute-done.10.refs_1_.refs_3_) | copy-start | bytes 1769476
  269.4 15.7 %copy-start.11 = (bf16[288,1024]{1,0:T(8,128)(2,1)}, bf16[288,1024]{1,0:T(8,128)(2,1)S(1)}, u32[]{:S(2)}) copy-start(bf16[288,1024]{1,0:T(8,128)(2,1)S(1)} %collective-permute-done.11.refs_2_.refs_4_) | copy-start | bytes 1769476
  271.7 14.0 %collective-permute-start.21 = (bf16[576,1024]{1,0:T(8,128)(2,1)}, bf16[576,1024]{1,0:T(8,128)(2,1)}, u32[]{:S(2)}, u32[]{:S(2)}) collective-permute-start(bf16[576,1024]{1,0:T(8,128)(2,1)} %get-tuple-element.234), channel_id=1, source_target_pairs={{0,1},{1,0},{2,3},{3,2},{4,5},{5,4},{6,7},{7,6},{8,9},{9,8},{10,11... | collective-permute-start | bytes 3538952 | tf_op jit(solution)/shard_map/ppermute | solution.py:986
  285.1 7.8 %collective-permute-start.22 = (bf16[16,128,512]{2,1,0:T(8,128)(2,1)}, bf16[16,128,512]{2,1,0:T(8,128)(2,1)S(1)}, u32[]{:S(2)}, u32[]{:S(2)}) collective-permute-start(bf16[16,128,512]{2,1,0:T(8,128)(2,1)} %get-tuple-element.243), channel_id=1, source_target_pairs={{0,1},{1,0},{2,3},{3,2},{4,5},{5,4},{6,7},{7,6},{8,9},{9,8},{10,11... | collective-permute-start | bytes 6291464 | tf_op jit(solution)/shard_map/ppermute | solution.py:986
  285.6 7.3 %collective-permute-start.23 = (bf16[16,128,512]{2,1,0:T(8,128)(2,1)}, bf16[16,128,512]{2,1,0:T(8,128)(2,1)}, u32[]{:S(2)}, u32[]{:S(2)}) collective-permute-start(bf16[16,128,512]{2,1,0:T(8,128)(2,1)} %get-tuple-element.245), channel_id=1, source_target_pairs={{0,1},{1,0},{2,3},{3,2},{4,5},{5,4},{6,7},{7,6},{8,9},{9,8},{10,11... | collective-permute-start | bytes 6291464 | tf_op jit(solution)/shard_map/ppermute | solution.py:986
  304.4 21.4 %collective-permute-start.26 = (bf16[8,128,512]{2,1,0:T(8,128)(2,1)S(1)}, bf16[8,128,512]{2,1,0:T(8,128)(2,1)S(1)}, u32[]{:S(2)}, u32[]{:S(2)}) collective-permute-start(bf16[8,128,512]{2,1,0:T(8,128)(2,1)S(1)} %bitcast.73), channel_id=1, source_target_pairs={{0,2},{1,3},{2,0},{3,1},{4,6},{5,7},{6,4},{7,5},{8,10},{9,11},{10,... | collective-permute-start | bytes 3145736 | tf_op jit(solution)/shard_map/ppermute | solution.py:986
  305.0 21.7 %collective-permute-start.27 = (bf16[8,128,512]{2,1,0:T(8,128)(2,1)S(1)}, bf16[8,128,512]{2,1,0:T(8,128)(2,1)S(1)}, u32[]{:S(2)}, u32[]{:S(2)}) collective-permute-start(bf16[8,128,512]{2,1,0:T(8,128)(2,1)S(1)} %bitcast.72), channel_id=1, source_target_pairs={{0,8},{8,0},{16,24},{24,16},{1,9},{9,1},{17,25},{25,17},{2,10},{10... | collective-permute-start | bytes 3145736 | tf_op jit(solution)/shard_map/ppermute | solution.py:986
  328.2 15.7 %collective-permute-start.34 = (bf16[4,128,512]{2,1,0:T(8,128)(2,1)S(1)}, bf16[4,128,512]{2,1,0:T(8,128)(2,1)S(1)}, u32[]{:S(2)}, u32[]{:S(2)}) collective-permute-start(bf16[4,128,512]{2,1,0:T(8,128)(2,1)S(1)} %bitcast.75), channel_id=1, source_target_pairs={{0,8},{8,0},{16,24},{24,16},{1,9},{9,1},{17,25},{25,17},{2,10},{10... | collective-permute-start | bytes 1572872 | tf_op jit(solution)/shard_map/ppermute | solution.py:986
  330.0 13.9 %collective-permute-start.35 = (bf16[4,128,512]{2,1,0:T(8,128)(2,1)S(1)}, bf16[4,128,512]{2,1,0:T(8,128)(2,1)S(1)}, u32[]{:S(2)}, u32[]{:S(2)}) collective-permute-start(bf16[4,128,512]{2,1,0:T(8,128)(2,1)S(1)} %bitcast.74), channel_id=1, source_target_pairs={{0,16},{8,24},{16,0},{24,8},{1,17},{9,25},{17,1},{25,9},{2,18},{10... | collective-permute-start | bytes 1572872 | tf_op jit(solution)/shard_map/ppermute | solution.py:986
  332.0 9.9 %collective-permute-start.28 = (f32[4,1024]{1,0:T(4,128)S(1)}, f32[4,1024]{1,0:T(4,128)S(1)}, u32[]{:S(2)}, u32[]{:S(2)}) collective-permute-start(f32[4,1024]{1,0:T(4,128)S(1)} %get-tuple-element.261.refs_0_), channel_id=1, source_target_pairs={{0,8},{8,0},{16,24},{24,16},{1,9},{9,1},{17,25},{25,17},{2,10},{10... | collective-permute-start | bytes 49160 | tf_op jit(solution)/shard_map/ppermute | solution.py:986
  332.4 9.5 %collective-permute-start.29 = (f32[4,1024]{1,0:T(4,128)S(1)}, f32[4,1024]{1,0:T(4,128)S(1)}, u32[]{:S(2)}, u32[]{:S(2)}) collective-permute-start(f32[4,1024]{1,0:T(4,128)S(1)} %get-tuple-element.261.refs_0_), channel_id=1, source_target_pairs={{0,16},{8,24},{16,0},{24,8},{1,17},{9,25},{17,1},{25,9},{2,18},{10... | collective-permute-start | bytes 49160 | tf_op jit(solution)/shard_map/ppermute | solution.py:986
  333.8 8.1 %collective-permute-start.30 = (f32[4,1024]{1,0:T(4,128)S(1)}, f32[4,1024]{1,0:T(4,128)S(1)}, u32[]{:S(2)}, u32[]{:S(2)}) collective-permute-start(f32[4,1024]{1,0:T(4,128)S(1)} %get-tuple-element.261.refs_0_), channel_id=1, source_target_pairs={{0,24},{8,16},{16,8},{24,0},{1,25},{9,17},{17,9},{25,1},{2,26},{10... | collective-permute-start | bytes 49160 | tf_op jit(solution)/shard_map/ppermute | solution.py:986
  341.9 11.4 %collective-permute-start.31 = (f32[4,1024]{1,0:T(4,128)S(1)}, f32[4,1024]{1,0:T(4,128)S(1)}, u32[]{:S(2)}, u32[]{:S(2)}) collective-permute-start(f32[4,1024]{1,0:T(4,128)S(1)} %get-tuple-element.266.refs_0_), channel_id=1, source_target_pairs={{0,1},{1,0},{2,3},{3,2},{4,5},{5,4},{6,7},{7,6},{8,9},{9,8},{10,11... | collective-permute-start | bytes 49160 | tf_op jit(solution)/shard_map/ppermute | solution.py:986
  342.0 11.3 %collective-permute-start.32 = (f32[4,1024]{1,0:T(4,128)S(1)}, f32[4,1024]{1,0:T(4,128)S(1)}, u32[]{:S(2)}, u32[]{:S(2)}) collective-permute-start(f32[4,1024]{1,0:T(4,128)S(1)} %get-tuple-element.266.refs_0_), channel_id=1, source_target_pairs={{0,2},{1,3},{2,0},{3,1},{4,6},{5,7},{6,4},{7,5},{8,10},{9,11},{10,... | collective-permute-start | bytes 49160 | tf_op jit(solution)/shard_map/ppermute | solution.py:986
  343.7 9.6 %collective-permute-start.33 = (f32[4,1024]{1,0:T(4,128)S(1)}, f32[4,1024]{1,0:T(4,128)S(1)}, u32[]{:S(2)}, u32[]{:S(2)}) collective-permute-start(f32[4,1024]{1,0:T(4,128)S(1)} %get-tuple-element.266.refs_0_), channel_id=1, source_target_pairs={{0,3},{1,2},{2,1},{3,0},{4,7},{5,6},{6,5},{7,4},{8,11},{9,10},{10,... | collective-permute-start | bytes 49160 | tf_op jit(solution)/shard_map/ppermute | solution.py:986
  344.0 11.3 %collective-permute-start.37 = (bf16[2,128,512]{2,1,0:T(8,128)(2,1)S(1)}, bf16[2,128,512]{2,1,0:T(8,128)(2,1)S(1)}, u32[]{:S(2)}, u32[]{:S(2)}) collective-permute-start(bf16[2,128,512]{2,1,0:T(8,128)(2,1)S(1)} %bitcast.77), channel_id=1, source_target_pairs={{0,16},{8,24},{16,0},{24,8},{1,17},{9,25},{17,1},{25,9},{2,18},{10... | collective-permute-start | bytes 786440 | tf_op jit(solution)/shard_map/ppermute | solution.py:986
  345.5 9.8 %collective-permute-start.38 = (bf16[2,128,512]{2,1,0:T(8,128)(2,1)S(1)}, bf16[2,128,512]{2,1,0:T(8,128)(2,1)S(1)}, u32[]{:S(2)}, u32[]{:S(2)}) collective-permute-start(bf16[2,128,512]{2,1,0:T(8,128)(2,1)S(1)} %bitcast.76), channel_id=1, source_target_pairs={{0,2},{1,3},{2,0},{3,1},{4,6},{5,7},{6,4},{7,5},{8,10},{9,11},{10,... | collective-permute-start | bytes 786440 | tf_op jit(solution)/shard_map/ppermute | solution.py:986
  353.3 4.7 %collective-permute-start.36 = (f32[4,1024]{1,0:T(4,128)S(1)}, f32[4,1024]{1,0:T(4,128)S(1)}, u32[]{:S(2)}, u32[]{:S(2)}) collective-permute-start(f32[4,1024]{1,0:T(4,128)S(1)} %get-tuple-element.277.refs_0_), channel_id=1, source_target_pairs={{0,4},{1,5},{2,6},{3,7},{4,0},{5,1},{6,2},{7,3},{8,12},{9,13},{10,... | collective-permute-start | bytes 49160 | tf_op jit(solution)/shard_map/ppermute | solution.py:986
  355.4 14.3 %collective-permute-start.39 = (bf16[1,128,1024]{2,1,0:T(8,128)(2,1)S(1)}, bf16[1,128,1024]{2,1,0:T(8,128)(2,1)S(1)}, u32[]{:S(2)}, u32[]{:S(2)}) collective-permute-start(bf16[1,128,1024]{2,1,0:T(8,128)(2,1)S(1)} %bitcast.78), channel_id=1, source_target_pairs={{0,4},{1,5},{2,6},{3,7},{4,0},{5,1},{6,2},{7,3},{8,12},{9,13},{10,... | collective-permute-start | bytes 786440 | tf_op jit(solution)/shard_map/ppermute | solution.py:986
where the time goes:
time: 375 us; the launch traced here: 372 us
  Pallas kernels  293 us (78%)
  starting transfers between devices  42.3 us (11%)
  waiting for transfers between devices  30.7 us (8%)
    pallas_call x46, Pallas kernels, apply(): *results, token = run(*args, *[far(a) for a in after], *order)  293 us
    ppermute x40, starting transfers between devices, swap(): return lax.ppermute(value, axis, [(i, i ^ mask) for i in range(size)])  42.3 us
    ppermute x40, waiting for transfers between devices, swap(): return lax.ppermute(value, axis, [(i, i ^ mask) for i in range(size)])  30.7 us
  transfers between devices with their start and end apart: 40, of which 10 were waited for; matrix products, arithmetic and copies ran while one was open for 0% of the time, Pallas kernels for 77%

commit v1 on v0

--- a/solution.py
+++ b/solution.py
@@ -1163,12 +1163,11 @@
     sums = stack_sums(sums_one, sums_two)
     sums_got = send_sums(0)
     d_w_out = finish(keep_out[0], got_out[0], last[0], 0, True, 0)
-    d_w_out = finish(keep_out[1], got_out[1], last[1], 0, True, 1, d_w_out)
     sums = add_rows([sums, *sums_got])
     one_step(2)
     sums_got = send_sums(1)
+    d_w_out = finish(keep_out[1], got_out[1], last[1], 0, True, 1, d_w_out)
     d_w_in = finish(keep_in[0], got_in[0], last[0], 1, False, 0)
-    d_w_in = finish(keep_in[1], got_in[1], last[1], 1, False, 1, d_w_in)
     sums = add_rows([sums, *sums_got])
     pairs = [state[side][:2] for side in sides]
     left = state[0][2]
@@ -1179,6 +1178,8 @@
         pairs = [(add_half(sets, 0)[0], got)]
         left = left[:at] + left[at + 1 :]
         sums_got = send_sums(number) if number < len(rounds) else []
+        if number == 2:
+            d_w_in = finish(keep_in[1], got_in[1], last[1], 1, False, 1, d_w_in)
         sums = add_rows([sums, *sums_got])
     value = pairs[0][0][0].astype(F32) + pairs[0][1][0].astype(F32)
     d_w_qkv = value[:own_qkv].T

time: 375 us -> 373 us (level)
  transfers between devices with their start and end apart: 40 -> 40, of which waited for: 10 -> 11; matrix products, arithmetic and copies ran while one was open for 0% -> 0% of each run, Pallas kernels for 77% -> 78%
where the time goes in v1:
time: 373 us; the launch traced here: 369 us
  Pallas kernels  293 us (79%)
  starting transfers between devices  41.1 us (11%)
  waiting for transfers between devices  29.9 us (8%)
    pallas_call x46, Pallas kernels, apply(): *results, token = run(*args, *[far(a) for a in after], *order)  293 us
    ppermute x40, starting transfers between devices, swap(): return lax.ppermute(value, axis, [(i, i ^ mask) for i in range(size)])  41.1 us
    ppermute x40, waiting for transfers between devices, swap(): return lax.ppermute(value, axis, [(i, i ^ mask) for i in range(size)])  29.9 us
  transfers between devices with their start and end apart: 40, of which 11 were waited for; matrix products, arithmetic and copies ran while one was open for 0% of the time, Pallas kernels for 78%

profile of v1, /device:TPU:0, one launch (start us, length us, event | category | flops | bytes accessed | tf_op | source)
XLA Modules:
  0.0 369.4 jit_solution(13384744439753387756)
XLA Ops:
  1.9 3.9 %shard_map.179 = (bf16[288,1024]{1,0:T(8,128)(2,1)}, bf16[288,1024]{1,0:T(8,128)(2,1)}, bf16[288,1024]{1,0:T(8,128)(2,1)}, bf16[288,1024]{1,0:T(8,128)(2,1)}, f32[8,128]{1,0:T(8,128)S(1)}) custom-call(s32[1,1024]{1,0:T(1,128)S(1)} %bitcast.69, bf16[1024,1024]{1,0:T(8,128)(2,1)} %refs_2_.7), custom_call_target="tpu_custom_call" | custom-call | flops 1 | tf_op jit(solution)/shard_map/pallas_call | solution.py:74
  5.8 2.3 shard_map.180
  8.1 3.0 collective-permute-start.2
  11.1 2.6 collective-permute-start.3
  13.9 4.7 %shard_map.181 = (bf16[1024,1024]{1,0:T(8,128)(2,1)}, f32[8,128]{1,0:T(8,128)S(1)}) custom-call(bf16[1024,1024]{1,0:T(8,128)(2,1)} %refs_0_.7, f32[2,1024]{1,0:T(2,128)} %refs_4_.7, f32[2,1024]{1,0:T(2,128)} %refs_4_.5, f32[8,128]{1,0:T(8,128)S(1)} %get-tuple-element.154.refs_3_), custom_call_target="tpu_custom_call" | custom-call | flops 1 | tf_op jit(solution)/shard_map/pallas_call | solution.py:74
  18.6 10.7 %shard_map.182 = (bf16[1024,3072]{1,0:T(8,128)(2,1)}, f32[8,128]{1,0:T(8,128)S(1)}) custom-call(bf16[1024,1024]{1,0:T(8,128)(2,1)} %get-tuple-element.155.refs_0_.refs_3_, bf16[1024,3072]{1,0:T(8,128)(2,1)} %refs_3_.7, f32[8,128]{1,0:T(8,128)S(1)} %get-tuple-element.156.refs_2_), custom_call_target="tpu_custom_call" | custom-call | flops 1 | tf_op jit(solution)/shard_map/pallas_call | solution.py:74
  29.3 18.5 %shard_map.183 = (bf16[1024,1024]{1,0:T(8,128)(2,1)S(1)}, bf16[1024,1024]{1,0:T(8,128)(2,1)}, f32[8,2,1024]{2,1,0:T(2,128)}, f32[8,128]{1,0:T(8,128)S(1)}) custom-call(s32[1024,1]{1,0:T(8,128)S(1)} %copy.38.refs_0_, bf16[1024,3072]{1,0:T(8,128)(2,1)} %get-tuple-element.157.refs_1_.refs_2_.refs_3_, ...), custom_call_target="tpu_custom_call" | custom-call | flops 1 | tf_op jit(solution)/shard_map/pallas_call | solution.py:74
  47.8 7.2 %shard_map.184 = (f32[1024,1024]{1,0:T(8,128)}, bf16[896,1024]{1,0:T(8,128)(2,1)S(1)}, f32[8,128]{1,0:T(8,128)S(1)}) custom-call(bf16[1024,1024]{1,0:T(8,128)(2,1)} %refs_0_.7, bf16[1024,1024]{1,0:T(8,128)(2,1)S(1)} %get-tuple-element.159.refs_1_.refs_4_, bf16[1024,1024]{1,0:T(8,128)(2,1)} %refs_3_.6, f32[2,1024]{1,0:T(2,128)} %refs_4_.7, ...), custom_call_target="tpu_custom_call" | custom-call | flops 1 | tf_op jit(solution)/shard_map/pallas_call | solution.py:74
  55.0 9.4 %shard_map.185 = (bf16[1152,4096]{1,0:T(8,128)(2,1)}, f32[8,128]{1,0:T(8,128)S(1)}) custom-call(bf16[4096,1024]{1,0:T(8,128)(2,1)} %bitcast.83, bf16[288,1024]{1,0:T(8,128)(2,1)S(1)} %copy-done.1, bf16[288,1024]{1,0:T(8,128)(2,1)S(1)} %collective-permute-done.2.refs_2_.refs_7_.refs_1_, f32[8,128]{1,0:T(8,128)S(1)} %get-tuple-element.166.refs_3_), custom_call_target="tpu_custom_call" | custom-call | flops 1 | tf_op jit(solution)/shard_map/pallas_call | solution.py:74
  64.4 2.9 shard_map.186
  67.8 2.6 shard_map.187
  71.2 1.0 collective-permute-start.9
  72.2 3.4 collective-permute-start.8
  75.6 9.5 %shard_map.189 = (bf16[1152,4096]{1,0:T(8,128)(2,1)}, f32[8,128]{1,0:T(8,128)S(1)}) custom-call(bf16[4096,1024]{1,0:T(8,128)(2,1)} %bitcast.84, bf16[288,1024]{1,0:T(8,128)(2,1)} %collective-permute-done.3.refs_8_.refs_1_.refs_2_, bf16[288,1024]{1,0:T(8,128)(2,1)} %collective-permute-done.4.refs_9_.refs_2_.refs_3_, ...), custom_call_target="tpu_custom_call", output_to_operand_aliasing={{0}: (3, {})} | custom-call | flops 1 | tf_op jit(solution)/shard_map/pallas_call | solution.py:74
  85.2 3.3 shard_map.190
  88.5 12.0 %shard_map.191 = (bf16[1152,4096]{1,0:T(8,128)(2,1)}, bf16[1152,4096]{1,0:T(8,128)(2,1)}, bf16[288,1024]{1,0:T(8,128)(2,1)}, f32[8,128]{1,0:T(8,128)S(1)}) custom-call(bf16[1024,4096]{1,0:T(8,128)(2,1)} %bitcast.79, bf16[1152,4096]{1,0:T(8,128)(2,1)} %get-tuple-element.179.refs_1_, bf16[288,1024]{1,0:T(8,128)(2,1)S(1)} %get-tuple-element.183.refs_2_.refs_0_, ...), custom_call_target="tpu_custom_call" | custom-call | flops 1 | tf_op jit(solution)/shard_map/pallas_call | solution.py:74
  100.4 11.8 %shard_map.192 = (bf16[1152,4096]{1,0:T(8,128)(2,1)}, bf16[1152,4096]{1,0:T(8,128)(2,1)}, bf16[288,1024]{1,0:T(8,128)(2,1)}, f32[8,128]{1,0:T(8,128)S(1)}) custom-call(bf16[1024,4096]{1,0:T(8,128)(2,1)} %bitcast.80, bf16[1152,4096]{1,0:T(8,128)(2,1)} %get-tuple-element.179.refs_1_, ...), custom_call_target="tpu_custom_call", output_to_operand_aliasing={{0}: (3, {}), {1}: (4, {})} | custom-call | flops 1 | tf_op jit(solution)/shard_map/pallas_call | solution.py:74
  112.8 2.3 collective-permute-done.8.refs_2_
  115.1 11.7 %shard_map.193 = (bf16[1152,4096]{1,0:T(8,128)(2,1)}, bf16[1152,4096]{1,0:T(8,128)(2,1)}, bf16[288,1024]{1,0:T(8,128)(2,1)}, f32[8,128]{1,0:T(8,128)S(1)}) custom-call(bf16[1024,4096]{1,0:T(8,128)(2,1)} %bitcast.81, bf16[1152,4096]{1,0:T(8,128)(2,1)} %get-tuple-element.179.refs_1_, ...), custom_call_target="tpu_custom_call", output_to_operand_aliasing={{0}: (3, {}), {1}: (4, {})} | custom-call | flops 1 | tf_op jit(solution)/shard_map/pallas_call | solution.py:74
  126.8 1.7 collective-permute-start.14
  128.5 12.4 %shard_map.194 = (bf16[1152,4096]{1,0:T(8,128)(2,1)}, bf16[1152,4096]{1,0:T(8,128)(2,1)}, bf16[288,1024]{1,0:T(8,128)(2,1)}, f32[8,128]{1,0:T(8,128)S(1)}) custom-call(bf16[1024,4096]{1,0:T(8,128)(2,1)} %bitcast.82, bf16[1152,4096]{1,0:T(8,128)(2,1)} %get-tuple-element.179.refs_1_, ...), custom_call_target="tpu_custom_call", output_to_operand_aliasing={{0}: (3, {}), {1}: (4, {})} | custom-call | flops 1 | tf_op jit(solution)/shard_map/pallas_call | solution.py:74
  140.9 1.0 collective-permute-start.15
  141.8 13.8 %shard_map.195 = (bf16[2,512,1024]{2,1,0:T(8,128)(2,1)}, bf16[2,512,1024]{2,1,0:T(8,128)(2,1)}, bf16[2,512,1024]{2,1,0:T(8,128)(2,1)}, bf16[2,512,1024]{2,1,0:T(8,128)(2,1)}, f32[8,128]{1,0:T(8,128)S(1)}) custom-call(s32[4]{0:T(128)S(1)} %broadcast_xor_fusion.refs_0_, bf16[1024,1152]{1,0:T(8,128)(2,1)} %get-tuple-element.196.refs_1_, ...), custom_call_target="tpu_custom_call" | custom-call | flops 1 | tf_op jit(solution)/shard_map/pallas_call | solution.py:74
  155.7 1.5 collective-permute-start.17
  157.2 1.5 collective-permute-start.18
  158.7 6.8 %shard_map.196 = (bf16[2,512,1024]{2,1,0:T(8,128)(2,1)}, bf16[2,512,1024]{2,1,0:T(8,128)(2,1)}, f32[8,128]{1,0:T(8,128)S(1)}) custom-call(s32[4]{0:T(128)S(1)} %broadcast_xor_fusion.refs_0_, bf16[1024,1152]{1,0:T(8,128)(2,1)} %get-tuple-element.196.refs_1_, ...), custom_call_target="tpu_custom_call", output_to_operand_aliasing={{0}: (3, {}), {1}: (4, {})} | custom-call | flops 1 | tf_op jit(solution)/shard_map/pallas_call | solution.py:74
  165.5 16.1 %shard_map.197 = (bf16[288,1024]{1,0:T(8,128)(2,1)S(1)}, bf16[288,1024]{1,0:T(8,128)(2,1)}, bf16[288,1024]{1,0:T(8,128)(2,1)}, bf16[288,1024]{1,0:T(8,128)(2,1)}, f32[8,128]{1,0:T(8,128)S(1)}) custom-call(bf16[1152,4096]{1,0:T(8,128)(2,1)} %get-tuple-element.195.refs_2_.refs_0_, bf16[4096,1024]{1,0:T(8,128)(2,1)} %bitcast.85, ...), custom_call_target="tpu_custom_call" | custom-call | flops 1 | tf_op jit(solution)/shard_map/pallas_call | solution.py:74
  181.6 2.1 shard_map.198
  183.7 16.7 %shard_map.199 = (bf16[2,512,1024]{2,1,0:T(8,128)(2,1)}, bf16[2,512,1024]{2,1,0:T(8,128)(2,1)}, bf16[2,512,1024]{2,1,0:T(8,128)(2,1)}, bf16[2,512,1024]{2,1,0:T(8,128)(2,1)}, f32[8,128]{1,0:T(8,128)S(1)}) custom-call(s32[4]{0:T(128)S(1)} %broadcast_xor_fusion.refs_0_, bf16[1024,1152]{1,0:T(8,128)(2,1)} %get-tuple-element.212.refs_1_, ...), custom_call_target="tpu_custom_call" | custom-call | flops 1 | tf_op jit(solution)/shard_map/pallas_call | solution.py:74
  201.5 1.2 shard_map.200
  202.8 2.8 collective-permute-done.16.refs_9_
  205.6 1.0 collective-permute-start.10
  206.6 2.5 collective-permute-start.11
  210.7 12.6 %shard_map.201 = (f32[1024,1024]{1,0:T(8,128)}, bf16[1024,1024]{1,0:T(8,128)(2,1)}, bf16[1024,1024]{1,0:T(8,128)(2,1)}, f32[2,1024]{1,0:T(2,128)S(1)}, f32[8,128]{1,0:T(8,128)S(1)}) custom-call(s32[1024,1]{1,0:T(8,128)S(1)} %copy.42.refs_0_, f32[1024,1024]{1,0:T(8,128)} %get-tuple-element.168.refs_1_, bf16[1024,1024]{1,0:T(8,128)(2,1)} %refs_2_.7, ...), custom_call_target="tpu_custom_call" | custom-call | flops 1 | tf_op jit(solution)/shard_map/pallas_call | solution.py:74
  223.3 22.2 %shard_map.202 = (bf16[3,1024,1024]{2,1,0:T(8,128)(2,1)}, bf16[3,1024,1024]{2,1,0:T(8,128)(2,1)}, f32[8,128]{1,0:T(8,128)S(1)}) custom-call(s32[1024,1]{1,0:T(8,128)S(1)} %copy.38.refs_0_, bf16[1024,3072]{1,0:T(8,128)(2,1)} %get-tuple-element.157.refs_1_.refs_2_.refs_3_, bf16[1024,3072]{1,0:T(8,128)(2,1)} %get-tuple-element.157.refs_1_.refs_2_.refs_3_, ...), custom_call_target="tpu_custom_call" | custom-call | flops 1 | tf_op jit(solution)/shard_map/pallas_call | solution.py:74
  246.4 1.2 collective-permute-done.20.refs_7_.refs_1_
  247.6 5.3 %shard_map.203 = (bf16[2,544,1024]{2,1,0:T(8,128)(2,1)}, bf16[2,544,1024]{2,1,0:T(8,128)(2,1)}, f32[8,128]{1,0:T(8,128)S(1)}) custom-call(bf16[2,512,1024]{2,1,0:T(8,128)(2,1)} %get-tuple-element.225.refs_0_, bf16[2,512,1024]{2,1,0:T(8,128)(2,1)} %copy-done.13, bf16[2,512,1024]{2,1,0:T(8,128)(2,1)} %get-tuple-element.226.refs_2_.refs_0_, ...), custom_call_target="tpu_custom_call" | custom-call | flops 1 | tf_op jit(solution)/shard_map/pallas_call | solution.py:74
  252.8 1.5 collective-permute-start.24
  254.9 14.4 %shard_map.204 = (bf16[3,1024,1024]{2,1,0:T(8,128)(2,1)}, bf16[3,1024,1024]{2,1,0:T(8,128)(2,1)}, f32[8,128]{1,0:T(8,128)S(1)}) custom-call(s32[1024,1]{1,0:T(8,128)S(1)} %copy.38.refs_0_, bf16[1024,3072]{1,0:T(8,128)(2,1)} %get-tuple-element.157.refs_1_.refs_2_.refs_3_, ...), custom_call_target="tpu_custom_call", output_to_operand_aliasing={{0}: (8, {}), {1}: (9, {})} | custom-call | flops 1 | tf_op jit(solution)/shard_map/pallas_call | solution.py:74
  269.4 2.3 shard_map.205
  271.7 13.4 %shard_map.206 = (bf16[16,128,512]{2,1,0:T(8,128)(2,1)}, bf16[16,128,512]{2,1,0:T(8,128)(2,1)}, bf16[16,128,512]{2,1,0:T(8,128)(2,1)}, bf16[16,128,512]{2,1,0:T(8,128)(2,1)}, f32[8,128]{1,0:T(8,128)S(1)}) custom-call(s32[1]{0:T(128)} %bitcast.6.refs_0_, bf16[3072,1024]{1,0:T(8,128)(2,1)} %bitcast.86, bf16[1024,1024]{1,0:T(8,128)(2,1)} %get-tuple-element.236.refs_2_, ...), custom_call_target="tpu_custom_call" | custom-call | flops 1 | tf_op jit(solution)/shard_map/pallas_call | solution.py:74
  285.7 7.2 %shard_map.207 = (bf16[1024,1024]{1,0:T(8,128)(2,1)}, f32[8,128]{1,0:T(8,128)S(1)}) custom-call(s32[1024,1]{1,0:T(8,128)S(1)} %copy.42.refs_0_, f32[1024,1024]{1,0:T(8,128)} %get-tuple-element.168.refs_1_, bf16[288,1024]{1,0:T(8,128)(2,1)} %copy-done.8, bf16[288,1024]{1,0:T(8,128)(2,1)} %copy-done.10, bf16[288,1024]{1,0:T(8,128)(2,1)} %copy-done.11, ...), custom_call_target="tpu_custom_call" | custom-call | flops 10350000128 | tf_op jit(solution)/shard_map/pallas_call | solution.py:74
  292.8 8.5 %collective-permute-done.24.refs_6_.refs_2_ = bf16[2,544,1024]{2,1,0:T(8,128)(2,1)} collective-permute-done((bf16[2,544,1024]{2,1,0:T(8,128)(2,1)}, bf16[2,544,1024]{2,1,0:T(8,128)(2,1)}, u32[]{:S(2)}, u32[]{:S(2)}) %collective-permute-start.24) | collective-permute-done | bytes 2228256 | tf_op jit(solution)/shard_map/ppermute | solution.py:986
  301.4 0.9 collective-permute-done.25.refs_7_.refs_2_
  302.3 2.1 shard_map.208
  305.0 1.5 collective-permute-start.27
  306.5 3.3 shard_map.209
  309.7 14.2 %shard_map.210 = (f32[1024,1024]{1,0:T(8,128)}, f32[2,1024]{1,0:T(2,128)S(1)}, f32[8,128]{1,0:T(8,128)S(1)}) custom-call(bf16[1024,1024]{1,0:T(8,128)(2,1)} %refs_0_.7, f32[1024,1024]{1,0:T(8,128)} %get-tuple-element.240.refs_1_, bf16[3,1024,1024]{2,1,0:T(8,128)(2,1)} %get-tuple-element.241.refs_2_, bf16[1024,3072]{1,0:T(8,128)(2,1)} %refs_3_.7, ...), custom_call_target="tpu_custom_call" | custom-call | flops 1 | tf_op jit(solution)/shard_map/pallas_call | solution.py:74
  324.0 1.9 collective-permute-done.26
  326.7 1.4 shard_map.211
  328.2 1.8 collective-permute-start.34
  330.5 1.4 shard_map.212
  332.4 1.4 collective-permute-start.29
  333.8 1.7 collective-permute-start.30
  335.5 3.2 shard_map.214
  338.8 1.6 collective-permute-done.29.refs_2_
  340.5 1.5 collective-permute-start.32
  343.2 1.5 collective-permute-start.38
  344.8 3.2 shard_map.218
  348.0 3.0 shard_map.219
  351.0 2.2 collective-permute-start.36
  353.4 1.3 collective-permute-start.39
  354.6 3.0 shard_map.223
  358.9 8.8 %collective-permute-done.39 = bf16[1,128,1024]{2,1,0:T(8,128)(2,1)S(1)} collective-permute-done((bf16[1,128,1024]{2,1,0:T(8,128)(2,1)S(1)}, bf16[1,128,1024]{2,1,0:T(8,128)(2,1)S(1)}, u32[]{:S(2)}, u32[]{:S(2)}) %collective-permute-start.39) | collective-permute-done | bytes 262176 | tf_op jit(solution)/shard_map/ppermute | solution.py:986
  (109 shorter events, 14.9 us)
Async XLA Ops:
  0.6 5.2 %collective-permute-start.1 = (bf16[1024,1024]{1,0:T(8,128)(2,1)}, bf16[1024,1024]{1,0:T(8,128)(2,1)S(1)}, u32[]{:S(2)}, u32[]{:S(2)}) collective-permute-start(bf16[1024,1024]{1,0:T(8,128)(2,1)} %refs_2_.7), channel_id=1, source_target_pairs={{0,1},{1,0},{2,3},{3,2},{4,5},{5,4},{6,7},{7,6},{8,9},{9,8},{10,11... | collective-permute-start | bytes 6291464 | tf_op jit(solution)/shard_map/ppermute | solution.py:986
  1.9 3.9 %collective-permute-start = (s32[1,1024]{1,0:T(1,128)S(1)}, s32[1,1024]{1,0:T(1,128)S(1)}, u32[]{:S(2)}, u32[]{:S(2)}) collective-permute-start(s32[1,1024]{1,0:T(1,128)S(1)} %bitcast.99), channel_id=1, source_target_pairs={{0,1},{1,0},{2,3},{3,2},{4,5},{5,4},{6,7},{7,6},{8,9},{9,8},{10,11... | collective-permute-start | bytes 12296 | tf_op jit(solution)/shard_map/ppermute | solution.py:986
  5.8 7.9 %copy-start.15 = (s32[1,1024]{1,0:T(1,128)S(1)}, s32[1,1024]{1,0:T(1,128)}, u32[]{:S(2)}) copy-start(s32[1,1024]{1,0:T(1,128)} %param.19) | copy-start | bytes 12292
  8.1 46.8 %collective-permute-start.2 = (bf16[288,1024]{1,0:T(8,128)(2,1)}, bf16[288,1024]{1,0:T(8,128)(2,1)S(1)}, u32[]{:S(2)}, u32[]{:S(2)}) collective-permute-start(bf16[288,1024]{1,0:T(8,128)(2,1)} %get-tuple-element.163), channel_id=1, source_target_pairs={{0,2},{1,3},{2,0},{3,1},{4,6},{5,7},{6,4},{7,5},{8,10},{9,11},{10,... | collective-permute-start | bytes 1769480 | tf_op jit(solution)/shard_map/ppermute | solution.py:986
  11.1 53.3 %collective-permute-start.3 = (bf16[288,1024]{1,0:T(8,128)(2,1)}, bf16[288,1024]{1,0:T(8,128)(2,1)}, u32[]{:S(2)}, u32[]{:S(2)}) collective-permute-start(bf16[288,1024]{1,0:T(8,128)(2,1)} %get-tuple-element.164), channel_id=1, source_target_pairs={{0,4},{1,5},{2,6},{3,7},{4,0},{5,1},{6,2},{7,3},{8,12},{9,13},{10,... | collective-permute-start | bytes 1769480 | tf_op jit(solution)/shard_map/ppermute | solution.py:986
  13.7 50.7 %collective-permute-start.4 = (bf16[288,1024]{1,0:T(8,128)(2,1)}, bf16[288,1024]{1,0:T(8,128)(2,1)}, u32[]{:S(2)}, u32[]{:S(2)}) collective-permute-start(bf16[288,1024]{1,0:T(8,128)(2,1)} %get-tuple-element.165), channel_id=1, source_target_pairs={{0,6},{1,7},{2,4},{3,5},{4,2},{5,3},{6,0},{7,1},{8,14},{9,15},{10,... | collective-permute-start | bytes 1769480 | tf_op jit(solution)/shard_map/ppermute | solution.py:986
  47.8 16.6 %copy-start = (bf16[1024,1024]{1,0:T(8,128)(2,1)}, bf16[1024,1024]{1,0:T(8,128)(2,1)S(1)}, u32[]{:S(2)}) copy-start(bf16[1024,1024]{1,0:T(8,128)(2,1)S(1)} %get-tuple-element.159.refs_1_.refs_4_) | copy-start | bytes 6291460
  47.8 7.2 %copy-start.1 = (bf16[288,1024]{1,0:T(8,128)(2,1)S(1)}, bf16[288,1024]{1,0:T(8,128)(2,1)}, u32[]{:S(2)}) copy-start(bf16[288,1024]{1,0:T(8,128)(2,1)} %get-tuple-element.162.refs_1_.refs_6_.refs_0_) | copy-start | bytes 1769476
  54.9 12.8 %collective-permute-start.6 = (bf16[896,1024]{1,0:T(8,128)(2,1)S(1)}, bf16[896,1024]{1,0:T(8,128)(2,1)S(1)}, u32[]{:S(2)}, u32[]{:S(2)}) collective-permute-start(bf16[896,1024]{1,0:T(8,128)(2,1)S(1)} %get-tuple-element.171.refs_2_), channel_id=1, source_target_pairs={{0,1},{1,0},{2,3},{3,2},{4,5},{5,4},{6,7},{7,6},{8,9},{9,8},{10,11... | collective-permute-start | bytes 5505032 | tf_op jit(solution)/shard_map/ppermute | solution.py:986
  54.9 9.4 %copy-start.3 = (bf16[288,1024]{1,0:T(8,128)(2,1)}, bf16[288,1024]{1,0:T(8,128)(2,1)S(1)}, u32[]{:S(2)}) copy-start(bf16[288,1024]{1,0:T(8,128)(2,1)S(1)} %collective-permute-done.2.refs_2_.refs_7_.refs_1_) | copy-start | bytes 1769476
  67.2 3.1 collective-permute-start.5
  71.2 29.3 %collective-permute-start.9 = (bf16[288,1024]{1,0:T(8,128)(2,1)S(1)}, bf16[288,1024]{1,0:T(8,128)(2,1)S(1)}, u32[]{:S(2)}, u32[]{:S(2)}) collective-permute-start(bf16[288,1024]{1,0:T(8,128)(2,1)S(1)} %get-tuple-element.182), channel_id=1, source_target_pairs={{0,2},{1,3},{2,0},{3,1},{4,6},{5,7},{6,4},{7,5},{8,10},{9,11},{10,... | collective-permute-start | bytes 1769480 | tf_op jit(solution)/shard_map/ppermute | solution.py:986
  72.2 42.9 %collective-permute-start.8 = (bf16[288,1024]{1,0:T(8,128)(2,1)S(1)}, bf16[288,1024]{1,0:T(8,128)(2,1)S(1)}, u32[]{:S(2)}, u32[]{:S(2)}) collective-permute-start(bf16[288,1024]{1,0:T(8,128)(2,1)S(1)} %get-tuple-element.181), channel_id=1, source_target_pairs={{0,4},{1,5},{2,6},{3,7},{4,0},{5,1},{6,2},{7,3},{8,12},{9,13},{10,... | collective-permute-start | bytes 1769480 | tf_op jit(solution)/shard_map/ppermute | solution.py:986
  75.6 52.9 %collective-permute-start.7 = (bf16[288,1024]{1,0:T(8,128)(2,1)S(1)}, bf16[288,1024]{1,0:T(8,128)(2,1)S(1)}, u32[]{:S(2)}, u32[]{:S(2)}) collective-permute-start(bf16[288,1024]{1,0:T(8,128)(2,1)S(1)} %get-tuple-element.180), channel_id=1, source_target_pairs={{0,6},{1,7},{2,4},{3,5},{4,2},{5,3},{6,0},{7,1},{8,14},{9,15},{10,... | collective-permute-start | bytes 1769480 | tf_op jit(solution)/shard_map/ppermute | solution.py:986
  75.6 9.5 %copy-start.2 = (bf16[288,1024]{1,0:T(8,128)(2,1)S(1)}, bf16[288,1024]{1,0:T(8,128)(2,1)}, u32[]{:S(2)}) copy-start(bf16[288,1024]{1,0:T(8,128)(2,1)} %get-tuple-element.162.refs_1_.refs_6_.refs_0_) | copy-start | bytes 1769476
  75.6 9.5 %copy-start.4 = (bf16[288,1024]{1,0:T(8,128)(2,1)S(1)}, bf16[288,1024]{1,0:T(8,128)(2,1)}, u32[]{:S(2)}) copy-start(bf16[288,1024]{1,0:T(8,128)(2,1)} %copy-done.3) | copy-start | bytes 1769476
  112.2 88.2 %collective-permute-start.13 = (bf16[288,1024]{1,0:T(8,128)(2,1)}, bf16[288,1024]{1,0:T(8,128)(2,1)}, u32[]{:S(2)}, u32[]{:S(2)}) collective-permute-start(bf16[288,1024]{1,0:T(8,128)(2,1)} %get-tuple-element.208), channel_id=1, source_target_pairs={{0,2},{1,3},{2,0},{3,1},{4,6},{5,7},{6,4},{7,5},{8,10},{9,11},{10,... | collective-permute-start | bytes 1769480 | tf_op jit(solution)/shard_map/ppermute | solution.py:986
  126.8 74.1 %collective-permute-start.14 = (bf16[288,1024]{1,0:T(8,128)(2,1)}, bf16[288,1024]{1,0:T(8,128)(2,1)}, u32[]{:S(2)}, u32[]{:S(2)}) collective-permute-start(bf16[288,1024]{1,0:T(8,128)(2,1)} %get-tuple-element.209), channel_id=1, source_target_pairs={{0,4},{1,5},{2,6},{3,7},{4,0},{5,1},{6,2},{7,3},{8,12},{9,13},{10,... | collective-permute-start | bytes 1769480 | tf_op jit(solution)/shard_map/ppermute | solution.py:986
  128.5 12.4 %copy-start.5 = (bf16[288,1024]{1,0:T(8,128)(2,1)}, bf16[288,1024]{1,0:T(8,128)(2,1)S(1)}, u32[]{:S(2)}) copy-start(bf16[288,1024]{1,0:T(8,128)(2,1)S(1)} %collective-permute-done.7.refs_2_.refs_3_) | copy-start | bytes 1769476
  128.5 13.3 %copy-start.16 = (s32[4]{0:T(128)S(1)}, s32[4]{0:T(128)}, u32[]{:S(2)}) copy-start(s32[4]{0:T(128)} %constant.32.clone) | copy-start | bytes 52
  140.9 60.6 %collective-permute-start.15 = (bf16[288,1024]{1,0:T(8,128)(2,1)}, bf16[288,1024]{1,0:T(8,128)(2,1)}, u32[]{:S(2)}, u32[]{:S(2)}) collective-permute-start(bf16[288,1024]{1,0:T(8,128)(2,1)} %get-tuple-element.210), channel_id=1, source_target_pairs={{0,6},{1,7},{2,4},{3,5},{4,2},{5,3},{6,0},{7,1},{8,14},{9,15},{10,... | collective-permute-start | bytes 1769480 | tf_op jit(solution)/shard_map/ppermute | solution.py:986
  155.7 50.9 %collective-permute-start.17 = (bf16[2,512,1024]{2,1,0:T(8,128)(2,1)}, bf16[2,512,1024]{2,1,0:T(8,128)(2,1)S(1)}, u32[]{:S(2)}, u32[]{:S(2)}) collective-permute-start(bf16[2,512,1024]{2,1,0:T(8,128)(2,1)} %get-tuple-element.217), channel_id=1, source_target_pairs={{0,8},{8,0},{16,24},{24,16},{1,9},{9,1},{17,25},{25,17},{2,10},{10... | collective-permute-start | bytes 6291464 | tf_op jit(solution)/shard_map/ppermute | solution.py:986
  157.2 52.0 %collective-permute-start.18 = (bf16[2,512,1024]{2,1,0:T(8,128)(2,1)}, bf16[2,512,1024]{2,1,0:T(8,128)(2,1)S(1)}, u32[]{:S(2)}, u32[]{:S(2)}) collective-permute-start(bf16[2,512,1024]{2,1,0:T(8,128)(2,1)} %get-tuple-element.218), channel_id=1, source_target_pairs={{0,16},{8,24},{16,0},{24,8},{1,17},{9,25},{17,1},{25,9},{2,18},{10... | collective-permute-start | bytes 6291464 | tf_op jit(solution)/shard_map/ppermute | solution.py:986
  165.5 16.2 %copy-start.6 = (bf16[288,1024]{1,0:T(8,128)(2,1)S(1)}, bf16[288,1024]{1,0:T(8,128)(2,1)}, u32[]{:S(2)}) copy-start(bf16[288,1024]{1,0:T(8,128)(2,1)} %copy-done.5) | copy-start | bytes 1769476
  181.6 2.1 copy-start.8
  183.7 17.8 %copy-start.7 = (bf16[288,1024]{1,0:T(8,128)(2,1)S(1)}, bf16[288,1024]{1,0:T(8,128)(2,1)}, u32[]{:S(2)}) copy-start(bf16[288,1024]{1,0:T(8,128)(2,1)} %get-tuple-element.207.refs_0_.refs_5_) | copy-start | bytes 1769476
  200.4 45.9 %collective-permute-start.19 = (bf16[2,512,1024]{2,1,0:T(8,128)(2,1)}, bf16[2,512,1024]{2,1,0:T(8,128)(2,1)}, u32[]{:S(2)}, u32[]{:S(2)}) collective-permute-start(bf16[2,512,1024]{2,1,0:T(8,128)(2,1)} %get-tuple-element.227), channel_id=1, source_target_pairs={{0,8},{8,0},{16,24},{24,16},{1,9},{9,1},{17,25},{25,17},{2,10},{10... | collective-permute-start | bytes 6291464 | tf_op jit(solution)/shard_map/ppermute | solution.py:986
  201.0 46.6 %collective-permute-start.20 = (bf16[2,512,1024]{2,1,0:T(8,128)(2,1)}, bf16[2,512,1024]{2,1,0:T(8,128)(2,1)}, u32[]{:S(2)}, u32[]{:S(2)}) collective-permute-start(bf16[2,512,1024]{2,1,0:T(8,128)(2,1)} %get-tuple-element.230), channel_id=1, source_target_pairs={{0,16},{8,24},{16,0},{24,8},{1,17},{9,25},{17,1},{25,9},{2,18},{10... | collective-permute-start | bytes 6291464 | tf_op jit(solution)/shard_map/ppermute | solution.py:986
  202.7 2.9 collective-permute-start.16
  205.6 4.4 %copy-start.14 = (bf16[576,1024]{1,0:T(8,128)(2,1)}, bf16[576,1024]{1,0:T(8,128)(2,1)S(1)}, u32[]{:S(2)}) copy-start(bf16[576,1024]{1,0:T(8,128)(2,1)S(1)} %collective-permute-done.16.refs_9_) | copy-start | bytes 3538948
  205.6 63.7 %collective-permute-start.10 = (bf16[288,1024]{1,0:T(8,128)(2,1)}, bf16[288,1024]{1,0:T(8,128)(2,1)S(1)}, u32[]{:S(2)}, u32[]{:S(2)}) collective-permute-start(bf16[288,1024]{1,0:T(8,128)(2,1)} %get-tuple-element.203), channel_id=1, source_target_pairs={{0,2},{1,3},{2,0},{3,1},{4,6},{5,7},{6,4},{7,5},{8,10},{9,11},{10,... | collective-permute-start | bytes 1769480 | tf_op jit(solution)/shard_map/ppermute | solution.py:986
  206.6 3.4 copy-start.13
  206.6 62.8 %collective-permute-start.11 = (bf16[288,1024]{1,0:T(8,128)(2,1)}, bf16[288,1024]{1,0:T(8,128)(2,1)S(1)}, u32[]{:S(2)}, u32[]{:S(2)}) collective-permute-start(bf16[288,1024]{1,0:T(8,128)(2,1)} %get-tuple-element.204), channel_id=1, source_target_pairs={{0,4},{1,5},{2,6},{3,7},{4,0},{5,1},{6,2},{7,3},{8,12},{9,13},{10,... | collective-permute-start | bytes 1769480 | tf_op jit(solution)/shard_map/ppermute | solution.py:986
  209.1 1.3 copy-start.12
  209.1 60.3 %collective-permute-start.12 = (bf16[288,1024]{1,0:T(8,128)(2,1)}, bf16[288,1024]{1,0:T(8,128)(2,1)}, u32[]{:S(2)}, u32[]{:S(2)}) collective-permute-start(bf16[288,1024]{1,0:T(8,128)(2,1)} %get-tuple-element.205), channel_id=1, source_target_pairs={{0,6},{1,7},{2,4},{3,5},{4,2},{5,3},{6,0},{7,1},{8,14},{9,15},{10,... | collective-permute-start | bytes 1769480 | tf_op jit(solution)/shard_map/ppermute | solution.py:986
  252.8 48.5 %collective-permute-start.24 = (bf16[2,544,1024]{2,1,0:T(8,128)(2,1)}, bf16[2,544,1024]{2,1,0:T(8,128)(2,1)}, u32[]{:S(2)}, u32[]{:S(2)}) collective-permute-start(bf16[2,544,1024]{2,1,0:T(8,128)(2,1)} %get-tuple-element.246), channel_id=1, source_target_pairs={{0,16},{8,24},{16,0},{24,8},{1,17},{9,25},{17,1},{25,9},{2,18},{10... | collective-permute-start | bytes 6684680 | tf_op jit(solution)/shard_map/ppermute | solution.py:986
  254.4 47.9 %collective-permute-start.25 = (bf16[2,544,1024]{2,1,0:T(8,128)(2,1)}, bf16[2,544,1024]{2,1,0:T(8,128)(2,1)}, u32[]{:S(2)}, u32[]{:S(2)}) collective-permute-start(bf16[2,544,1024]{2,1,0:T(8,128)(2,1)} %get-tuple-element.247), channel_id=1, source_target_pairs={{0,8},{8,0},{16,24},{24,16},{1,9},{9,1},{17,25},{25,17},{2,10},{10... | collective-permute-start | bytes 6684680 | tf_op jit(solution)/shard_map/ppermute | solution.py:986
  254.9 14.5 %copy-start.9 = (bf16[288,1024]{1,0:T(8,128)(2,1)S(1)}, bf16[288,1024]{1,0:T(8,128)(2,1)}, u32[]{:S(2)}) copy-start(bf16[288,1024]{1,0:T(8,128)(2,1)} %copy-done.8) | copy-start | bytes 1769476
  269.4 15.7 %copy-start.10 = (bf16[288,1024]{1,0:T(8,128)(2,1)}, bf16[288,1024]{1,0:T(8,128)(2,1)S(1)}, u32[]{:S(2)}) copy-start(bf16[288,1024]{1,0:T(8,128)(2,1)S(1)} %collective-permute-done.10.refs_1_.refs_3_) | copy-start | bytes 1769476
  269.4 15.7 %copy-start.11 = (bf16[288,1024]{1,0:T(8,128)(2,1)}, bf16[288,1024]{1,0:T(8,128)(2,1)S(1)}, u32[]{:S(2)}) copy-start(bf16[288,1024]{1,0:T(8,128)(2,1)S(1)} %collective-permute-done.11.refs_2_.refs_4_) | copy-start | bytes 1769476
  271.7 14.0 %collective-permute-start.21 = (bf16[576,1024]{1,0:T(8,128)(2,1)}, bf16[576,1024]{1,0:T(8,128)(2,1)}, u32[]{:S(2)}, u32[]{:S(2)}) collective-permute-start(bf16[576,1024]{1,0:T(8,128)(2,1)} %get-tuple-element.234), channel_id=1, source_target_pairs={{0,1},{1,0},{2,3},{3,2},{4,5},{5,4},{6,7},{7,6},{8,9},{9,8},{10,11... | collective-permute-start | bytes 3538952 | tf_op jit(solution)/shard_map/ppermute | solution.py:986
  285.1 7.8 %collective-permute-start.22 = (bf16[16,128,512]{2,1,0:T(8,128)(2,1)}, bf16[16,128,512]{2,1,0:T(8,128)(2,1)S(1)}, u32[]{:S(2)}, u32[]{:S(2)}) collective-permute-start(bf16[16,128,512]{2,1,0:T(8,128)(2,1)} %get-tuple-element.243), channel_id=1, source_target_pairs={{0,1},{1,0},{2,3},{3,2},{4,5},{5,4},{6,7},{7,6},{8,9},{9,8},{10,11... | collective-permute-start | bytes 6291464 | tf_op jit(solution)/shard_map/ppermute | solution.py:986
  285.6 7.3 %collective-permute-start.23 = (bf16[16,128,512]{2,1,0:T(8,128)(2,1)}, bf16[16,128,512]{2,1,0:T(8,128)(2,1)}, u32[]{:S(2)}, u32[]{:S(2)}) collective-permute-start(bf16[16,128,512]{2,1,0:T(8,128)(2,1)} %get-tuple-element.245), channel_id=1, source_target_pairs={{0,1},{1,0},{2,3},{3,2},{4,5},{5,4},{6,7},{7,6},{8,9},{9,8},{10,11... | collective-permute-start | bytes 6291464 | tf_op jit(solution)/shard_map/ppermute | solution.py:986
  304.4 21.4 %collective-permute-start.26 = (bf16[8,128,512]{2,1,0:T(8,128)(2,1)S(1)}, bf16[8,128,512]{2,1,0:T(8,128)(2,1)S(1)}, u32[]{:S(2)}, u32[]{:S(2)}) collective-permute-start(bf16[8,128,512]{2,1,0:T(8,128)(2,1)S(1)} %bitcast.73), channel_id=1, source_target_pairs={{0,2},{1,3},{2,0},{3,1},{4,6},{5,7},{6,4},{7,5},{8,10},{9,11},{10,... | collective-permute-start | bytes 3145736 | tf_op jit(solution)/shard_map/ppermute | solution.py:986
  305.0 21.7 %collective-permute-start.27 = (bf16[8,128,512]{2,1,0:T(8,128)(2,1)S(1)}, bf16[8,128,512]{2,1,0:T(8,128)(2,1)S(1)}, u32[]{:S(2)}, u32[]{:S(2)}) collective-permute-start(bf16[8,128,512]{2,1,0:T(8,128)(2,1)S(1)} %bitcast.72), channel_id=1, source_target_pairs={{0,8},{8,0},{16,24},{24,16},{1,9},{9,1},{17,25},{25,17},{2,10},{10... | collective-permute-start | bytes 3145736 | tf_op jit(solution)/shard_map/ppermute | solution.py:986
  328.2 14.2 %collective-permute-start.34 = (bf16[4,128,512]{2,1,0:T(8,128)(2,1)S(1)}, bf16[4,128,512]{2,1,0:T(8,128)(2,1)S(1)}, u32[]{:S(2)}, u32[]{:S(2)}) collective-permute-start(bf16[4,128,512]{2,1,0:T(8,128)(2,1)S(1)} %bitcast.75), channel_id=1, source_target_pairs={{0,8},{8,0},{16,24},{24,16},{1,9},{9,1},{17,25},{25,17},{2,10},{10... | collective-permute-start | bytes 1572872 | tf_op jit(solution)/shard_map/ppermute | solution.py:986
  330.0 12.4 %collective-permute-start.35 = (bf16[4,128,512]{2,1,0:T(8,128)(2,1)S(1)}, bf16[4,128,512]{2,1,0:T(8,128)(2,1)S(1)}, u32[]{:S(2)}, u32[]{:S(2)}) collective-permute-start(bf16[4,128,512]{2,1,0:T(8,128)(2,1)S(1)} %bitcast.74), channel_id=1, source_target_pairs={{0,16},{8,24},{16,0},{24,8},{1,17},{9,25},{17,1},{25,9},{2,18},{10... | collective-permute-start | bytes 1572872 | tf_op jit(solution)/shard_map/ppermute | solution.py:986
  332.0 6.8 %collective-permute-start.28 = (f32[4,1024]{1,0:T(4,128)S(1)}, f32[4,1024]{1,0:T(4,128)S(1)}, u32[]{:S(2)}, u32[]{:S(2)}) collective-permute-start(f32[4,1024]{1,0:T(4,128)S(1)} %get-tuple-element.261.refs_0_), channel_id=1, source_target_pairs={{0,8},{8,0},{16,24},{24,16},{1,9},{9,1},{17,25},{25,17},{2,10},{10... | collective-permute-start | bytes 49160 | tf_op jit(solution)/shard_map/ppermute | solution.py:986
  332.4 8.1 %collective-permute-start.29 = (f32[4,1024]{1,0:T(4,128)S(1)}, f32[4,1024]{1,0:T(4,128)S(1)}, u32[]{:S(2)}, u32[]{:S(2)}) collective-permute-start(f32[4,1024]{1,0:T(4,128)S(1)} %get-tuple-element.261.refs_0_), channel_id=1, source_target_pairs={{0,16},{8,24},{16,0},{24,8},{1,17},{9,25},{17,1},{25,9},{2,18},{10... | collective-permute-start | bytes 49160 | tf_op jit(solution)/shard_map/ppermute | solution.py:986
  333.8 6.6 %collective-permute-start.30 = (f32[4,1024]{1,0:T(4,128)S(1)}, f32[4,1024]{1,0:T(4,128)S(1)}, u32[]{:S(2)}, u32[]{:S(2)}) collective-permute-start(f32[4,1024]{1,0:T(4,128)S(1)} %get-tuple-element.261.refs_0_), channel_id=1, source_target_pairs={{0,24},{8,16},{16,8},{24,0},{1,25},{9,17},{17,9},{25,1},{2,26},{10... | collective-permute-start | bytes 49160 | tf_op jit(solution)/shard_map/ppermute | solution.py:986
  340.4 10.6 %collective-permute-start.31 = (f32[4,1024]{1,0:T(4,128)S(1)}, f32[4,1024]{1,0:T(4,128)S(1)}, u32[]{:S(2)}, u32[]{:S(2)}) collective-permute-start(f32[4,1024]{1,0:T(4,128)S(1)} %get-tuple-element.264.refs_0_), channel_id=1, source_target_pairs={{0,1},{1,0},{2,3},{3,2},{4,5},{5,4},{6,7},{7,6},{8,9},{9,8},{10,11... | collective-permute-start | bytes 49160 | tf_op jit(solution)/shard_map/ppermute | solution.py:986
  340.5 10.5 %collective-permute-start.32 = (f32[4,1024]{1,0:T(4,128)S(1)}, f32[4,1024]{1,0:T(4,128)S(1)}, u32[]{:S(2)}, u32[]{:S(2)}) collective-permute-start(f32[4,1024]{1,0:T(4,128)S(1)} %get-tuple-element.264.refs_0_), channel_id=1, source_target_pairs={{0,2},{1,3},{2,0},{3,1},{4,6},{5,7},{6,4},{7,5},{8,10},{9,11},{10,... | collective-permute-start | bytes 49160 | tf_op jit(solution)/shard_map/ppermute | solution.py:986
  342.0 9.0 %collective-permute-start.33 = (f32[4,1024]{1,0:T(4,128)S(1)}, f32[4,1024]{1,0:T(4,128)S(1)}, u32[]{:S(2)}, u32[]{:S(2)}) collective-permute-start(f32[4,1024]{1,0:T(4,128)S(1)} %get-tuple-element.264.refs_0_), channel_id=1, source_target_pairs={{0,3},{1,2},{2,1},{3,0},{4,7},{5,6},{6,5},{7,4},{8,11},{9,10},{10,... | collective-permute-start | bytes 49160 | tf_op jit(solution)/shard_map/ppermute | solution.py:986
  342.5 10.7 %collective-permute-start.37 = (bf16[2,128,512]{2,1,0:T(8,128)(2,1)S(1)}, bf16[2,128,512]{2,1,0:T(8,128)(2,1)S(1)}, u32[]{:S(2)}, u32[]{:S(2)}) collective-permute-start(bf16[2,128,512]{2,1,0:T(8,128)(2,1)S(1)} %bitcast.77), channel_id=1, source_target_pairs={{0,16},{8,24},{16,0},{24,8},{1,17},{9,25},{17,1},{25,9},{2,18},{10... | collective-permute-start | bytes 786440 | tf_op jit(solution)/shard_map/ppermute | solution.py:986
  343.2 10.0 %collective-permute-start.38 = (bf16[2,128,512]{2,1,0:T(8,128)(2,1)S(1)}, bf16[2,128,512]{2,1,0:T(8,128)(2,1)S(1)}, u32[]{:S(2)}, u32[]{:S(2)}) collective-permute-start(bf16[2,128,512]{2,1,0:T(8,128)(2,1)S(1)} %bitcast.76), channel_id=1, source_target_pairs={{0,2},{1,3},{2,0},{3,1},{4,6},{5,7},{6,4},{7,5},{8,10},{9,11},{10,... | collective-permute-start | bytes 786440 | tf_op jit(solution)/shard_map/ppermute | solution.py:986
  351.0 6.6 %collective-permute-start.36 = (f32[4,1024]{1,0:T(4,128)S(1)}, f32[4,1024]{1,0:T(4,128)S(1)}, u32[]{:S(2)}, u32[]{:S(2)}) collective-permute-start(f32[4,1024]{1,0:T(4,128)S(1)} %get-tuple-element.275.refs_0_), channel_id=1, source_target_pairs={{0,4},{1,5},{2,6},{3,7},{4,0},{5,1},{6,2},{7,3},{8,12},{9,13},{10,... | collective-permute-start | bytes 49160 | tf_op jit(solution)/shard_map/ppermute | solution.py:986
  353.4 14.3 %collective-permute-start.39 = (bf16[1,128,1024]{2,1,0:T(8,128)(2,1)S(1)}, bf16[1,128,1024]{2,1,0:T(8,128)(2,1)S(1)}, u32[]{:S(2)}, u32[]{:S(2)}) collective-permute-start(bf16[1,128,1024]{2,1,0:T(8,128)(2,1)S(1)} %bitcast.78), channel_id=1, source_target_pairs={{0,4},{1,5},{2,6},{3,7},{4,0},{5,1},{6,2},{7,3},{8,12},{9,13},{10,... | collective-permute-start | bytes 786440 | tf_op jit(solution)/shard_map/ppermute | solution.py:986
